TPU v7x, 32 devices: a whole 2x2x4 slice. The times are simulated.
32 devices in a mesh: ctx: 4 (over z), fsdp: 8 (over y, x, core).
Axes of the slice: x: 2, y: 2, z: 4, core: 2. Of those that a mesh axis runs over, the one named last changes fastest.
Arguments:
- tokens: bfloat16 [8, 1024, 2048], P('fsdp', 'ctx'), may hold values from -6 to 6
- block_order: int32 [8, 4], P('fsdp'), may hold values from 0 to 3, each once within a row
- ln_gain: bfloat16 [2048], P('fsdp'), may hold values from 0.5 to 1.5
- ln_bias: bfloat16 [2048], P('fsdp'), may hold values from -2 to 2
- w_qkv: bfloat16 [2048, 6144], P('fsdp'), may hold values from -0.125 to 0.125
- w_out: bfloat16 [2048, 2048], P('fsdp'), may hold values from -2 to 2
- w_gate: bfloat16 [2048, 5632], P('fsdp'), may hold values from -0.125 to 0.125
- w_up: bfloat16 [2048, 5632], P('fsdp'), may hold values from -0.125 to 0.125
- w_down: bfloat16 [5632, 2048], P('fsdp'), may hold values from -0.109375 to 0.109375
- cotangent: bfloat16 [8, 1024, 2048], P('fsdp', 'ctx'), may hold values from -6 to 6
Outputs:
- out: bfloat16 [8, 1024, 2048], P('fsdp', 'ctx')
- grad_in: float32 [8, 1024, 2048], P('fsdp', 'ctx')
- d_gain: float32 [2048], P('fsdp')
- d_bias: float32 [2048], P('fsdp')
- d_qkv: float32 [2048, 6144], P('fsdp')
- d_out: float32 [2048, 2048], P('fsdp')
- d_gate: float32 [2048, 5632], P('fsdp')
- d_up: float32 [2048, 5632], P('fsdp')
- d_down: float32 [5632, 2048], P('fsdp')
Inputs may be any that keep to these rules, and one draw needn't show every extreme that they name: Each row of block_order holds every block number from 0 to 3 once.
All inputs are finite; a program needn't handle non-finite values.
Results may differ from a plain program's by a relative error of at most 0.018.
Values may be sent and summed in bfloat16 or wider, within the bound.
A program may use at most 512 MiB of HBM per device.

v0:
```python
import jax
import jax.numpy as jnp
from jax import lax
from jax.sharding import PartitionSpec as P

H = 32
HD = 64
ROT = 16


EPS = 1e-05
NEG = -1e30


def from_behind(value, axis, steps):
    count = lax.axis_size(axis)
    pairs = [(source, (source + steps) % count) for source in range(count)]
    return lax.ppermute(value, axis, pairs)


def angles(positions):
    half_rot = ROT // 2
    inverse = 10000.0 ** (-jnp.arange(half_rot, dtype=jnp.float32) / half_rot)
    angle_grid = positions.astype(jnp.float32)[:, None] * inverse[None, :]
    return (jnp.cos(angle_grid)[:, None, :], jnp.sin(angle_grid)[:, None, :])


def rotate(field, cosine, sine_table):
    half_rot = ROT // 2
    leading = field[..., :half_rot]
    trailing = field[..., half_rot:ROT]
    return jnp.concatenate(
        [
            leading * cosine - trailing * sine_table,
            trailing * cosine + leading * sine_table,
            field[..., ROT:],
        ],
        axis=-1,
    )


def unrotate(field, cosine, sine_table):
    half_rot = ROT // 2
    leading = field[..., :half_rot]
    trailing = field[..., half_rot:ROT]
    return jnp.concatenate(
        [
            leading * cosine + trailing * sine_table,
            trailing * cosine - leading * sine_table,
            field[..., ROT:],
        ],
        axis=-1,
    )


def project(xf, params, own_pos):
    gain, bias, w_qkv, w_out, w_gate, w_up, w_down = params
    row_count, model_width = xf.shape
    average = jnp.mean(xf, axis=-1, keepdims=True)
    centered = xf - average
    variance = jnp.mean(centered * centered, axis=-1, keepdims=True)
    inv_std = lax.rsqrt(variance + EPS)
    x_hat = centered * inv_std
    normed_low = (x_hat * gain.astype(jnp.float32) + bias.astype(jnp.float32)).astype(jnp.bfloat16)
    mixed_qkv = jnp.dot(normed_low, w_qkv, preferred_element_type=jnp.float32)
    cosine, sine_table = angles(own_pos)
    queries = rotate(
        mixed_qkv[:, :model_width].reshape(row_count, H, HD), cosine, sine_table
    ).astype(jnp.bfloat16)
    keys_low = rotate(
        mixed_qkv[:, model_width : 2 * model_width].reshape(row_count, H, HD), cosine, sine_table
    )
    keys_low = keys_low.astype(jnp.bfloat16).reshape(row_count, model_width)
    values_low = mixed_qkv[:, 2 * model_width :].astype(jnp.bfloat16)
    gate_value = jnp.dot(normed_low, w_gate, preferred_element_type=jnp.float32)
    up_value = jnp.dot(normed_low, w_up, preferred_element_type=jnp.float32)
    return (
        normed_low,
        x_hat,
        inv_std,
        queries,
        keys_low,
        values_low,
        gate_value,
        up_value,
        cosine,
        sine_table,
    )


def attend(queries, keys_low, values_low, own_pos, positions_all):
    row_count = queries.shape[0]
    score_scale = HD ** (-0.5)
    key_part = lax.all_gather(keys_low, "ctx", axis=0, tiled=True)
    value_part = lax.all_gather(values_low, "ctx", axis=0, tiled=True)
    piece_rows = key_part.shape[0]
    allowed = (positions_all[None, :] <= own_pos[:, None])[None]
    key_heads = key_part.reshape(piece_rows, H, HD)
    value_heads = value_part.reshape(piece_rows, H, HD)
    running_max = jnp.full((H, row_count), NEG, jnp.float32)
    scores = (
        jnp.einsum("qhd,khd->hqk", queries, key_heads, preferred_element_type=jnp.float32)
        * score_scale
    )
    scores = jnp.where(allowed, scores, NEG)
    new_max = jnp.maximum(running_max, jnp.max(scores, axis=-1))
    soft_weights = jnp.where(allowed, jnp.exp(scores - new_max[..., None]), 0.0)
    running_sum = jnp.sum(soft_weights, axis=-1)
    weighted = jnp.einsum(
        "hqk,khd->hqd",
        soft_weights.astype(jnp.bfloat16),
        value_heads,
        preferred_element_type=jnp.float32,
    )
    running_max, running_sum, weighted = (new_max, running_sum, weighted)
    attended = (weighted / running_sum[..., None]).transpose(1, 0, 2).reshape(row_count, H * HD)
    return (attended, running_max + jnp.log(running_sum))


def pass_keys(key_part, value_part):
    return from_behind((key_part, value_part), "ctx", 1)


def pass_grads(key_grad, value_grad):
    return (
        from_behind(key_grad.astype(jnp.bfloat16), "ctx", 1).astype(key_grad.dtype),
        from_behind(value_grad.astype(jnp.bfloat16), "ctx", 1).astype(value_grad.dtype),
    )


def attend_back(
    queries, keys_low, values_low, d_attended, log_total, row_delta, own_pos, positions_all
):
    row_count = queries.shape[0]
    model_width = keys_low.shape[1]
    context_size = lax.axis_size("ctx")
    place_index = lax.axis_index("ctx")
    score_scale = HD ** (-0.5)

    def visit_block(source, key_part, value_part, gradients):
        key_pos = lax.dynamic_slice_in_dim(positions_all, source * row_count, row_count)
        allowed = (key_pos[None, :] <= own_pos[:, None])[None]
        key_heads = key_part.reshape(row_count, H, HD)
        value_heads = value_part.reshape(row_count, H, HD)
        query_grad, key_grad, value_grad = gradients
        scores = (
            jnp.einsum("qhd,khd->hqk", queries, key_heads, preferred_element_type=jnp.float32)
            * score_scale
        )
        scores = jnp.where(allowed, scores, NEG)
        soft_weights = jnp.where(allowed, jnp.exp(scores - log_total[..., None]), 0.0)
        value_grad = value_grad + jnp.einsum(
            "hqk,qhd->khd",
            soft_weights.astype(jnp.bfloat16),
            d_attended,
            preferred_element_type=jnp.float32,
        ).reshape(row_count, model_width)
        d_prob = jnp.einsum(
            "qhd,khd->hqk", d_attended, value_heads, preferred_element_type=jnp.float32
        )
        d_score = (soft_weights * (d_prob - row_delta[..., None])).astype(jnp.bfloat16)
        query_grad = (
            query_grad
            + jnp.einsum("hqk,khd->qhd", d_score, key_heads, preferred_element_type=jnp.float32)
            * score_scale
        )
        key_grad = key_grad + (
            jnp.einsum("hqk,qhd->khd", d_score, queries, preferred_element_type=jnp.float32)
            * score_scale
        ).reshape(row_count, model_width)
        return (query_grad, key_grad, value_grad)

    zero_query = jnp.zeros((row_count, H, HD), jnp.float32)
    zero_keys = jnp.zeros((row_count, model_width), jnp.float32)
    query_grad, key_grad, value_grad = visit_block(
        place_index, keys_low, values_low, (zero_query, zero_keys, zero_keys)
    )

    def turn(turn_index, state):
        key_part, value_part, query_grad, key_grad, value_grad = state
        key_part, value_part = pass_keys(key_part, value_part)
        key_grad, value_grad = pass_grads(key_grad, value_grad)
        source = (place_index - turn_index) % context_size
        query_grad, key_grad, value_grad = visit_block(
            source, key_part, value_part, (query_grad, key_grad, value_grad)
        )
        return (key_part, value_part, query_grad, key_grad, value_grad)

    final = lax.fori_loop(
        1, context_size, turn, (keys_low, values_low, query_grad, key_grad, value_grad)
    )
    key_grad, value_grad = pass_grads(final[3], final[4])
    return (final[2], key_grad, value_grad)


def body(tokens, block_order, ln_gain, ln_bias, w_qkv, w_out, w_gate, w_up, w_down, cotangent):
    block_rows = tokens.shape[1]
    model_width = tokens.shape[2]
    place_index = lax.axis_index("ctx")
    block_ids = block_order[0]
    positions_all = (
        block_ids[:, None] * block_rows + jnp.arange(block_rows, dtype=jnp.int32)[None, :]
    ).reshape(-1)
    own_pos = lax.dynamic_slice_in_dim(positions_all, place_index * block_rows, block_rows)
    xf = tokens[0].astype(jnp.float32)
    shards = (ln_gain, ln_bias, w_qkv, w_out, w_gate, w_up, w_down)
    params = (
        lax.all_gather(shards[0], "fsdp", axis=0, tiled=True),
        lax.all_gather(shards[1], "fsdp", axis=0, tiled=True),
        lax.all_gather(shards[2], "fsdp", axis=0, tiled=True),
        lax.all_gather(shards[3], "fsdp", axis=0, tiled=True),
        lax.all_gather(shards[4], "fsdp", axis=0, tiled=True),
        lax.all_gather(shards[5], "fsdp", axis=0, tiled=True),
        lax.all_gather(shards[6], "fsdp", axis=0, tiled=True),
    )
    first_pass = project(xf, params, own_pos)
    attended, log_total = attend(
        first_pass[3], first_pass[4], first_pass[5], own_pos, positions_all
    )
    hidden = (jax.nn.silu(first_pass[6]) * first_pass[7]).astype(jnp.bfloat16)
    branch = jnp.dot(
        attended.astype(jnp.bfloat16), params[3], preferred_element_type=jnp.float32
    ) + jnp.dot(hidden, params[6], preferred_element_type=jnp.float32)
    out = (xf + branch).astype(jnp.bfloat16)[None]
    params = (
        lax.all_gather(shards[0], "fsdp", axis=0, tiled=True),
        lax.all_gather(shards[1], "fsdp", axis=0, tiled=True),
        lax.all_gather(shards[2], "fsdp", axis=0, tiled=True),
        lax.all_gather(shards[3], "fsdp", axis=0, tiled=True),
        lax.all_gather(shards[4], "fsdp", axis=0, tiled=True),
        lax.all_gather(shards[5], "fsdp", axis=0, tiled=True),
        lax.all_gather(shards[6], "fsdp", axis=0, tiled=True),
    )
    (
        normed_low,
        x_hat,
        inv_std,
        queries,
        keys_low,
        values_low,
        gate_value,
        up_value,
        cosine,
        sine_table,
    ) = project(xf, params, own_pos)
    attended, log_total = attend(queries, keys_low, values_low, own_pos, positions_all)
    attended_low = attended.astype(jnp.bfloat16)
    sigmoid_gate = jax.nn.sigmoid(gate_value)
    hidden = (gate_value * sigmoid_gate * up_value).astype(jnp.bfloat16)
    gain_all, bias_all, qkv_all, out_all, gate_all, up_all, down_all = params
    grad_low = cotangent[0]
    grad_out = grad_low.astype(jnp.float32)
    contract_rows = (((0,), (0,)), ((), ()))
    d_hidden = jnp.dot(grad_low, down_all.T, preferred_element_type=jnp.float32)
    d_gate_act = (
        d_hidden * up_value * sigmoid_gate * (1.0 + gate_value * (1.0 - sigmoid_gate))
    ).astype(jnp.bfloat16)
    d_up_act = (d_hidden * gate_value * sigmoid_gate).astype(jnp.bfloat16)
    d_inner = jnp.concatenate([d_gate_act, d_up_act], axis=1)
    hidden_width = w_gate.shape[1]
    part = hidden
    grad_down = lax.psum_scatter(
        lax.dot_general(part, grad_low, contract_rows, preferred_element_type=jnp.float32).astype(
            jnp.bfloat16
        ),
        "fsdp",
        scatter_dimension=0,
        tiled=True,
    )
    part = normed_low
    grad_inner = lax.psum_scatter(
        lax.dot_general(part, d_inner, contract_rows, preferred_element_type=jnp.float32).astype(
            jnp.bfloat16
        ),
        "fsdp",
        scatter_dimension=0,
        tiled=True,
    ).astype(jnp.float32)
    grad_gate = grad_inner[:, :hidden_width]
    grad_up = grad_inner[:, hidden_width:]
    d_normed = jnp.dot(d_gate_act, gate_all.T, preferred_element_type=jnp.float32) + jnp.dot(
        d_up_act, up_all.T, preferred_element_type=jnp.float32
    )
    row_count = xf.shape[0]
    d_attended = jnp.dot(grad_low, out_all.T, preferred_element_type=jnp.float32).astype(
        jnp.bfloat16
    )
    attended_heads = attended.reshape(row_count, H, HD)
    d_attended_heads = d_attended.reshape(row_count, H, HD)
    row_delta = jnp.sum(d_attended_heads.astype(jnp.float32) * attended_heads, axis=-1).T
    query_grad, key_grad, value_grad = attend_back(
        queries,
        keys_low,
        values_low,
        d_attended_heads,
        log_total,
        row_delta,
        own_pos,
        positions_all,
    )
    query_part = unrotate(query_grad, cosine, sine_table).reshape(row_count, model_width)
    key_part = unrotate(key_grad.reshape(row_count, H, HD), cosine, sine_table).reshape(
        row_count, model_width
    )
    d_mixed = jnp.concatenate([query_part, key_part, value_grad], axis=1).astype(jnp.bfloat16)
    full_qkv = lax.dot_general(
        normed_low, d_mixed, contract_rows, preferred_element_type=jnp.float32
    )
    full_out = lax.dot_general(
        attended_low, grad_low, contract_rows, preferred_element_type=jnp.float32
    )
    d_normed = d_normed + jnp.dot(d_mixed, qkv_all.T, preferred_element_type=jnp.float32)
    full_gain = jnp.sum(d_normed * x_hat, axis=0)
    full_bias = jnp.sum(d_normed, axis=0)
    scaled = d_normed * gain_all.astype(jnp.float32)
    d_input = inv_std * (
        scaled
        - jnp.mean(scaled, axis=-1, keepdims=True)
        - x_hat * jnp.mean(scaled * x_hat, axis=-1, keepdims=True)
    )
    grad_in = (grad_out + d_input)[None]
    grad_gain, grad_bias, grad_qkv, grad_outw = (
        lax.psum_scatter(
            full_gain.astype(jnp.bfloat16), "fsdp", scatter_dimension=0, tiled=True
        ).astype(jnp.float32),
        lax.psum_scatter(
            full_bias.astype(jnp.bfloat16), "fsdp", scatter_dimension=0, tiled=True
        ).astype(jnp.float32),
        lax.psum_scatter(
            full_qkv.astype(jnp.bfloat16), "fsdp", scatter_dimension=0, tiled=True
        ).astype(jnp.float32),
        lax.psum_scatter(
            full_out.astype(jnp.bfloat16), "fsdp", scatter_dimension=0, tiled=True
        ).astype(jnp.float32),
    )
    summed = (
        lax.psum(grad_gain.astype(jnp.bfloat16), "ctx").astype(jnp.float32),
        lax.psum(grad_bias.astype(jnp.bfloat16), "ctx").astype(jnp.float32),
        lax.psum(grad_qkv.astype(jnp.bfloat16), "ctx").astype(jnp.float32),
        lax.psum(grad_outw.astype(jnp.bfloat16), "ctx").astype(jnp.float32),
        lax.psum(grad_gate.astype(jnp.bfloat16), "ctx").astype(jnp.float32),
        lax.psum(grad_up.astype(jnp.bfloat16), "ctx").astype(jnp.float32),
        lax.psum(grad_down, "ctx").astype(jnp.float32),
    )
    return (out, grad_in) + tuple(summed)


def solution(mesh):
    return jax.shard_map(
        body,
        mesh=mesh,
        in_specs=(
            P("fsdp", "ctx", None),
            P("fsdp", None),
            P("fsdp"),
            P("fsdp"),
            P("fsdp", None),
            P("fsdp", None),
            P("fsdp", None),
            P("fsdp", None),
            P("fsdp", None),
            P("fsdp", "ctx", None),
        ),
        out_specs=(
            P("fsdp", "ctx", None),
            P("fsdp", "ctx", None),
            P("fsdp"),
            P("fsdp"),
            P("fsdp", None),
            P("fsdp", None),
            P("fsdp", None),
            P("fsdp", None),
            P("fsdp", None),
        ),
        check_vma=False,
    )
```

profile of v0, /device:TPU:0, one launch (start us, length us, event | category | flops | bytes accessed | tf_op | source)
XLA Modules:
  0.0 2099.6 jit_solution(4627962343365710167)
XLA Ops:
  10.7 10.3 all-gather.1
  21.1 8.9 all-gather
  30.6 107.3 %all-gather.10.cloned.1.call-done = bf16[2048,6144]{1,0:T(8,128)(2,1)} async-done(((bf16[256,6144]{1,0:T(8,128)(2,1)}), bf16[2048,6144]{1,0:T(8,128)(2,1)}) %all-gather.10.cloned.1.call-update) | async-done | bytes 25165840 | tf_op jit(solution)/shard_map/all_gather | solution.py:210
  138.0 11.7 fusion.63
  149.7 3.2 copy-done.8
  154.5 101.9 %all-gather.18.cloned.1.call-done = bf16[2048,5632]{1,0:T(8,128)(2,1)} async-done(((bf16[256,5632]{1,0:T(8,128)(2,1)}), bf16[2048,5632]{1,0:T(8,128)(2,1)}) %all-gather.18.cloned.1.call-update) | async-done | bytes 23068688 | tf_op jit(solution)/shard_map/all_gather | solution.py:212
  256.3 13.6 fusion.61
  269.9 104.8 %all-gather.20.cloned.1.call-done = bf16[2048,5632]{1,0:T(8,128)(2,1)} async-done(((bf16[256,5632]{1,0:T(8,128)(2,1)}), bf16[2048,5632]{1,0:T(8,128)(2,1)}) %all-gather.20.cloned.1.call-update) | async-done | bytes 23068688 | tf_op jit(solution)/shard_map/all_gather | solution.py:213
  374.8 13.8 fusion.59
  396.1 96.9 %all-gather.22.cloned.1.call-done = bf16[5632,2048]{1,0:T(8,128)(2,1)} async-done(((bf16[704,2048]{1,0:T(8,128)(2,1)}), bf16[5632,2048]{1,0:T(8,128)(2,1)}) %all-gather.22.cloned.1.call-update) | async-done | bytes 23068688 | tf_op jit(solution)/shard_map/all_gather | solution.py:214
  493.0 19.1 multiply_convert_fusion.2
  512.2 22.3 %convolution_convert_fusion = bf16[2048,11264]{1,0:T(8,128)(2,1)} fusion(bf16[256,5632]{1,0:T(8,128)(2,1)} %get-tuple-element.405, bf16[256,5632]{1,0:T(8,128)(2,1)} %get-tuple-element.406, bf16[1,256,2048]{2,1,0:T(8,128)(2,1)S(1)} %copy-done.2, f32[2048]{0:T(1024)S(1)} %bitcast.195, f32[2048]{0:T(1024)S(1)} %bitcast.188, f32[256]{0:T(256)S(1)} %add_rsqrt_fusion, ...), kind=kOutput, calls=%fused_computation.13 | convolution fusion | flops 11848908800 | bytes 52971520 | tf_op jit(solution)/shard_map/dot_general | solution.py:272
  534.8 14.4 all-gather.16.cloned.1.call-done
  549.2 6.7 convolution_convert_fusion.4
  564.2 67.2 %all-gather.14.cloned.1.call-done = bf16[1024,2048]{1,0:T(8,128)(2,1)} async-done(((bf16[256,2048]{1,0:T(8,128)(2,1)}), bf16[1024,2048]{1,0:T(8,128)(2,1)}) %all-gather.14.cloned.1.call-update) | async-done | bytes 4194320 | tf_op jit(solution)/shard_map/all_gather | solution.py:95
  631.4 6.4 copy.37
  637.8 74.3 %all-gather.12.cloned.1.call-done = bf16[1024,2048]{0,1:T(8,128)(2,1)} async-done(((bf16[256,2048]{0,1:T(8,128)(2,1)}), bf16[1024,2048]{0,1:T(8,128)(2,1)}) %all-gather.12.cloned.1.call-update) | async-done | bytes 4194320 | tf_op jit(solution)/shard_map/all_gather | solution.py:94
  712.1 17.5 fusion.7
  729.6 16.0 fusion.8
  745.6 19.6 multiply_reduce_fusion
  765.2 6.9 convolution_convert_fusion.3
  772.1 14.5 convolution_convert_fusion.1
  790.8 4.4 multiply_convert_fusion.1
  799.9 3.4 fusion.17
  803.2 288.8 %while.23 = (s32[]{:T(128)}, bf16[256,2048]{0,1:T(8,128)(2,1)}, bf16[256,2048]{0,1:T(8,128)(2,1)}, f32[256,32,64]{0,2,1:T(8,128)}, bf16[256,2048]{0,1:T(8,128)(2...) while((s32[]{:T(128)}, bf16[256,2048]{0,1:T(8,128)(2,1)}, ...), condition=%wide.region_6.7_spmd, body=%wide.region_5.6_spmd.sunk | while | flops 1372127232 | bytes 104108608 | solution.py:189
  804.2 4.0 collective-permute-start.3
  808.4 22.9 %collective-permute-done = bf16[256,2048]{0,1:T(8,128)(2,1)S(1)} collective-permute-done((bf16[256,2048]{0,1:T(8,128)(2,1)}, bf16[256,2048]{0,1:T(8,128)(2,1)S(1)}, u32[]{:S(2)}, u32[]{:S(2)}) %collective-permute-start) | collective-permute-done | bytes 1048608 | tf_op jit(solution)/shard_map/while/body/eval_jaxpr/ppermute | solution.py:18
  833.6 20.2 collective-permute-done.1
  854.7 4.5 multiply_convert_fusion.6
  860.1 16.3 collective-permute-done.2
  882.7 15.0 collective-permute-done.3
  901.1 4.2 collective-permute-start.3
  905.5 23.0 %collective-permute-done = bf16[256,2048]{0,1:T(8,128)(2,1)S(1)} collective-permute-done((bf16[256,2048]{0,1:T(8,128)(2,1)}, bf16[256,2048]{0,1:T(8,128)(2,1)S(1)}, u32[]{:S(2)}, u32[]{:S(2)}) %collective-permute-start) | collective-permute-done | bytes 1048608 | tf_op jit(solution)/shard_map/while/body/eval_jaxpr/ppermute | solution.py:18
  930.7 20.2 collective-permute-done.1
  951.9 4.5 multiply_convert_fusion.6
  957.3 16.3 collective-permute-done.2
  979.9 14.1 collective-permute-done.3
  997.4 4.1 collective-permute-start.3
  1001.8 23.0 %collective-permute-done = bf16[256,2048]{0,1:T(8,128)(2,1)S(1)} collective-permute-done((bf16[256,2048]{0,1:T(8,128)(2,1)}, bf16[256,2048]{0,1:T(8,128)(2,1)S(1)}, u32[]{:S(2)}, u32[]{:S(2)}) %collective-permute-start) | collective-permute-done | bytes 1048608 | tf_op jit(solution)/shard_map/while/body/eval_jaxpr/ppermute | solution.py:18
  1027.0 20.2 collective-permute-done.1
  1048.2 4.5 multiply_convert_fusion.6
  1053.5 16.3 collective-permute-done.2
  1076.1 13.2 collective-permute-done.3
  1093.7 26.5 %collective-permute-done.4 = bf16[256,2048]{0,1:T(8,128)(2,1)S(1)} collective-permute-done((bf16[256,2048]{0,1:T(8,128)(2,1)}, bf16[256,2048]{0,1:T(8,128)(2,1)S(1)}, u32[]{:S(2)}, u32[]{:S(2)}) %collective-permute-start.4) | collective-permute-done | bytes 1048608 | tf_op jit(solution)/shard_map/ppermute | solution.py:18
  1122.2 16.7 collective-permute-done.5
  1139.9 15.3 convolution_convert_fusion.2
  1157.1 91.0 %all-reduce.9.cloned.1.call-done = bf16[2048,11264]{1,0:T(8,128)(2,1)} async-done(((bf16[2048,11264]{1,0:T(8,128)(2,1)}), bf16[2048,11264]{1,0:T(8,128)(2,1)}) %all-reduce.9.cloned.1.call-update) | async-done | bytes 46137360
  1248.1 6.7 fusion.66
  1254.8 68.5 %reduce-scatter.6.cloned.1.call-done = bf16[256,2048]{1,0:T(8,128)(2,1)} async-done(((bf16[2048,2048]{1,0:T(8,128)(2,1)}), bf16[256,2048]{1,0:T(8,128)(2,1)}) %reduce-scatter.6.cloned.1.call-update) | async-done | bytes 1048592 | tf_op jit(solution)/shard_map/reduce_scatter | solution.py:332
  1323.3 149.4 %reduce-scatter.8.cloned.1.call-done = bf16[704,2048]{1,0:T(8,128)(2,1)} async-done(((bf16[5632,2048]{1,0:T(8,128)(2,1)}), bf16[704,2048]{1,0:T(8,128)(2,1)}) %reduce-scatter.8.cloned.1.call-update) | async-done | bytes 2883600 | tf_op jit(solution)/shard_map/reduce_scatter | solution.py:262
  1472.7 160.5 %reduce-scatter.4.cloned.1.call-done = bf16[256,6144]{1,0:T(8,128)(2,1)} async-done(((bf16[2048,6144]{1,0:T(8,128)(2,1)}), bf16[256,6144]{1,0:T(8,128)(2,1)}) %reduce-scatter.4.cloned.1.call-update) | async-done | bytes 3145744 | tf_op jit(solution)/shard_map/reduce_scatter | solution.py:329
  1633.2 12.5 fusion.70
  1645.8 13.1 convolution_add_fusion.1
  1658.9 5.9 fusion.69
  1664.8 12.3 fusion.29
  1677.1 14.1 fusion.37
  1691.2 13.9 all-reduce.3
  1705.2 13.7 all-reduce.4
  1720.1 3.7 fusion.36
  1723.8 351.1 %all-reduce.11.cloned.1.call-done = (bf16[256,6144]{1,0:T(8,128)(2,1)}, bf16[256,2048]{1,0:T(8,128)(2,1)}, bf16[256,5632]{1,0:T(8,128)(2,1)}, bf16[256,5632]{1,0:T(8,128)(2,1)}, bf16[704,2048]{1,0:T(8,128)(2,1)}) async-done(((bf16[256,6144]{1,0:T(8,128)(2,1)}, bf16[256,2048]{1,0:T(8,128)(2,1)}, bf16[256,5632]{1,0:T(8,128)(2,1)}, bf16[256,5632]{1,0:T(8,128)(2,1)}, bf16[704,2048]{1,0:T(8,128)(2,1)}), ...) | async-done | bytes 12845072 | tf_op jit(solution)/shard_map/psum | solution.py:339
  2074.9 5.4 convert_element_type.221
  2082.9 3.2 convert_element_type.225
  2086.1 3.2 convert_element_type.226
  2089.3 3.3 convert_element_type.228
  (196 shorter events, 82.6 us)
Async XLA Ops:
  7.2 130.8 %all-gather.10.cloned.1.call-start = ((), (), s32[]{:S(2)}) async-start(), calls=%async_computation.3 | async-start | bytes 28311552 | tf_op jit(solution)/shard_map/all_gather | solution.py:210
  7.9 248.4 %all-gather.18.cloned.1.call-start = ((), (), s32[]{:S(2)}) async-start(), calls=%async_computation.7 | async-start | bytes 25952256 | tf_op jit(solution)/shard_map/all_gather | solution.py:212
  8.7 2.0 copy-start.33
  8.7 12.4 copy-start.34
  8.7 21.3 %copy-start.2 = (bf16[1,256,2048]{2,1,0:T(8,128)(2,1)S(1)}, bf16[1,256,2048]{2,1,0:T(8,128)(2,1)}, u32[]{:S(2)}) copy-start(bf16[1,256,2048]{2,1,0:T(8,128)(2,1)} %param.12) | copy-start | bytes 3145732
  8.7 366.1 %all-gather.20.cloned.1.call-start = ((), (), s32[]{:S(2)}) async-start(), calls=%async_computation.8 | async-start | bytes 25952256 | tf_op jit(solution)/shard_map/all_gather | solution.py:213
  9.4 483.6 %all-gather.22.cloned.1.call-start = ((), (), s32[]{:S(2)}) async-start(), calls=%async_computation.9 | async-start | bytes 25952256 | tf_op jit(solution)/shard_map/all_gather | solution.py:214
  10.0 539.1 %all-gather.16.cloned.1.call-start = ((), (), s32[]{:S(2)}) async-start(), calls=%async_computation.6 | async-start | bytes 9437184 | tf_op jit(solution)/shard_map/all_gather | solution.py:211
  10.6 620.8 %all-gather.14.cloned.1.call-start = ((), (), s32[]{:S(2)}) async-start(), calls=%async_computation.5 | async-start | bytes 5242880 | tf_op jit(solution)/shard_map/all_gather | solution.py:95
  21.0 491.1 %copy-start.18 = (f32[8,1,256]{2,1,0:T(1,128)}, f32[8,1,256]{2,1,0:T(1,128)S(1)}, u32[]{:S(2)}) copy-start(f32[8,1,256]{2,1,0:T(1,128)S(1)} %convert_element_type.230) | copy-start | bytes 24580
  30.0 482.2 %copy-start.16 = (f32[8,1,256]{2,1,0:T(1,128)}, f32[8,1,256]{2,1,0:T(1,128)S(1)}, u32[]{:S(2)}) copy-start(f32[8,1,256]{2,1,0:T(1,128)S(1)} %convert_element_type.229) | copy-start | bytes 24580
  30.2 481.9 %copy-start.25 = (f32[256]{0:T(256)}, f32[256]{0:T(256)S(1)}, u32[]{:S(2)}) copy-start(f32[256]{0:T(256)S(1)} %broadcast_multiply_fusion.2) | copy-start | bytes 3076
  30.6 481.5 %copy-start.27 = (f32[256]{0:T(256)}, f32[256]{0:T(256)S(1)}, u32[]{:S(2)}) copy-start(f32[256]{0:T(256)S(1)} %add_rsqrt_fusion) | copy-start | bytes 3076
  149.7 3.2 copy-start.8
  154.1 558.0 %all-gather.12.cloned.1.call-start = ((), (), s32[]{:S(2)}) async-start(), calls=%async_computation.4 | async-start | bytes 5242880 | tf_op jit(solution)/shard_map/all_gather | solution.py:94
  154.5 408.6 %copy-start.29 = (f32[256,8]{0,1:T(8,128)}, f32[256,8]{0,1:T(8,128)S(1)}, u32[]{:S(2)}) copy-start(f32[256,8]{0,1:T(8,128)S(1)} %get-tuple-element.422) | copy-start | bytes 24580
  154.5 408.6 %copy-start.31 = (f32[256,8]{0,1:T(8,128)}, f32[256,8]{0,1:T(8,128)S(1)}, u32[]{:S(2)}) copy-start(f32[256,8]{0,1:T(8,128)S(1)} %get-tuple-element.423) | copy-start | bytes 24580
  374.8 13.8 copy-start.9
  395.8 852.3 %all-reduce.9.cloned.1.call-start = ((), (), s32[]{:S(2)}) async-start(), calls=%async_computation.13 | async-start | bytes 92274688
  534.5 14.7 copy-start.5
  534.5 788.8 %reduce-scatter.6.cloned.1.call-start = ((), (), s32[]{:S(2)}) async-start(), calls=%async_computation.11 | async-start | bytes 9437184 | tf_op jit(solution)/shard_map/reduce_scatter | solution.py:332
  772.1 700.6 %reduce-scatter.8.cloned.1.call-start = ((), (), s32[]{:S(2)}) async-start(), calls=%async_computation.12 | async-start | bytes 25952256 | tf_op jit(solution)/shard_map/reduce_scatter | solution.py:262
  786.7 846.5 %reduce-scatter.4.cloned.1.call-start = ((), (), s32[]{:S(2)}) async-start(), calls=%async_computation.10 | async-start | bytes 28311552 | tf_op jit(solution)/shard_map/reduce_scatter | solution.py:329
  789.3 1.5 copy-start.24
  803.2 28.1 %collective-permute-start = (bf16[256,2048]{0,1:T(8,128)(2,1)}, bf16[256,2048]{0,1:T(8,128)(2,1)S(1)}, u32[]{:S(2)}, u32[]{:S(2)}) collective-permute-start(bf16[256,2048]{0,1:T(8,128)(2,1)} %get-tuple-element.529), channel_id=1, source_target_pairs={{0,8},{8,16},{16,24},{24,0},{1,9},{9,17},{17,25},{25,1},{2,10},{10... | collective-permute-start | bytes 3145736 | tf_op jit(solution)/shard_map/while/body/eval_jaxpr/ppermute | solution.py:18
  803.2 50.5 %collective-permute-start.1 = (bf16[256,2048]{0,1:T(8,128)(2,1)}, bf16[256,2048]{0,1:T(8,128)(2,1)S(1)}, u32[]{:S(2)}, u32[]{:S(2)}) collective-permute-start(bf16[256,2048]{0,1:T(8,128)(2,1)} %get-tuple-element.530), channel_id=1, source_target_pairs={{0,8},{8,16},{16,24},{24,0},{1,9},{9,17},{17,25},{25,1},{2,10},{10... | collective-permute-start | bytes 3145736 | tf_op jit(solution)/shard_map/while/body/eval_jaxpr/ppermute | solution.py:18
  803.7 72.6 %collective-permute-start.2 = (bf16[256,2048]{0,1:T(8,128)(2,1)}, bf16[256,2048]{0,1:T(8,128)(2,1)}, u32[]{:S(2)}, u32[]{:S(2)}) collective-permute-start(bf16[256,2048]{0,1:T(8,128)(2,1)} %get-tuple-element.532), channel_id=1, source_target_pairs={{0,8},{8,16},{16,24},{24,0},{1,9},{9,17},{17,25},{25,1},{2,10},{10... | collective-permute-start | bytes 3145736 | tf_op jit(solution)/shard_map/while/body/eval_jaxpr/ppermute | solution.py:18
  804.2 93.5 %collective-permute-start.3 = (bf16[256,2048]{0,1:T(8,128)(2,1)}, bf16[256,2048]{0,1:T(8,128)(2,1)}, u32[]{:S(2)}, u32[]{:S(2)}) collective-permute-start(bf16[256,2048]{0,1:T(8,128)(2,1)} %get-tuple-element.533), channel_id=1, source_target_pairs={{0,8},{8,16},{16,24},{24,0},{1,9},{9,17},{17,25},{25,1},{2,10},{10... | collective-permute-start | bytes 3145736 | tf_op jit(solution)/shard_map/while/body/eval_jaxpr/ppermute | solution.py:18
  832.3 22.5 %copy-start.23 = (bf16[256,32,64]{0,2,1:T(8,128)(2,1)S(1)}, bf16[256,32,64]{0,2,1:T(8,128)(2,1)}, u32[]{:S(2)}) copy-start(bf16[256,32,64]{0,2,1:T(8,128)(2,1)} %get-tuple-element.558) | copy-start | bytes 3145732 | tf_op jit(solution)/shard_map/while
  860.1 19.0 copy-start
  880.5 2.2 copy-start.1
  900.4 28.1 %collective-permute-start = (bf16[256,2048]{0,1:T(8,128)(2,1)}, bf16[256,2048]{0,1:T(8,128)(2,1)S(1)}, u32[]{:S(2)}, u32[]{:S(2)}) collective-permute-start(bf16[256,2048]{0,1:T(8,128)(2,1)} %get-tuple-element.529), channel_id=1, source_target_pairs={{0,8},{8,16},{16,24},{24,0},{1,9},{9,17},{17,25},{25,1},{2,10},{10... | collective-permute-start | bytes 3145736 | tf_op jit(solution)/shard_map/while/body/eval_jaxpr/ppermute | solution.py:18
  900.4 50.6 %collective-permute-start.1 = (bf16[256,2048]{0,1:T(8,128)(2,1)}, bf16[256,2048]{0,1:T(8,128)(2,1)S(1)}, u32[]{:S(2)}, u32[]{:S(2)}) collective-permute-start(bf16[256,2048]{0,1:T(8,128)(2,1)} %get-tuple-element.530), channel_id=1, source_target_pairs={{0,8},{8,16},{16,24},{24,0},{1,9},{9,17},{17,25},{25,1},{2,10},{10... | collective-permute-start | bytes 3145736 | tf_op jit(solution)/shard_map/while/body/eval_jaxpr/ppermute | solution.py:18
  900.4 73.1 %collective-permute-start.2 = (bf16[256,2048]{0,1:T(8,128)(2,1)}, bf16[256,2048]{0,1:T(8,128)(2,1)}, u32[]{:S(2)}, u32[]{:S(2)}) collective-permute-start(bf16[256,2048]{0,1:T(8,128)(2,1)} %get-tuple-element.532), channel_id=1, source_target_pairs={{0,8},{8,16},{16,24},{24,0},{1,9},{9,17},{17,25},{25,1},{2,10},{10... | collective-permute-start | bytes 3145736 | tf_op jit(solution)/shard_map/while/body/eval_jaxpr/ppermute | solution.py:18
  901.1 92.8 %collective-permute-start.3 = (bf16[256,2048]{0,1:T(8,128)(2,1)}, bf16[256,2048]{0,1:T(8,128)(2,1)}, u32[]{:S(2)}, u32[]{:S(2)}) collective-permute-start(bf16[256,2048]{0,1:T(8,128)(2,1)} %get-tuple-element.533), channel_id=1, source_target_pairs={{0,8},{8,16},{16,24},{24,0},{1,9},{9,17},{17,25},{25,1},{2,10},{10... | collective-permute-start | bytes 3145736 | tf_op jit(solution)/shard_map/while/body/eval_jaxpr/ppermute | solution.py:18
  929.4 22.5 %copy-start.23 = (bf16[256,32,64]{0,2,1:T(8,128)(2,1)S(1)}, bf16[256,32,64]{0,2,1:T(8,128)(2,1)}, u32[]{:S(2)}) copy-start(bf16[256,32,64]{0,2,1:T(8,128)(2,1)} %get-tuple-element.558) | copy-start | bytes 3145732 | tf_op jit(solution)/shard_map/while
  957.2 19.0 copy-start
  977.6 2.2 copy-start.1
  996.6 28.1 %collective-permute-start = (bf16[256,2048]{0,1:T(8,128)(2,1)}, bf16[256,2048]{0,1:T(8,128)(2,1)S(1)}, u32[]{:S(2)}, u32[]{:S(2)}) collective-permute-start(bf16[256,2048]{0,1:T(8,128)(2,1)} %get-tuple-element.529), channel_id=1, source_target_pairs={{0,8},{8,16},{16,24},{24,0},{1,9},{9,17},{17,25},{25,1},{2,10},{10... | collective-permute-start | bytes 3145736 | tf_op jit(solution)/shard_map/while/body/eval_jaxpr/ppermute | solution.py:18
  996.6 50.6 %collective-permute-start.1 = (bf16[256,2048]{0,1:T(8,128)(2,1)}, bf16[256,2048]{0,1:T(8,128)(2,1)S(1)}, u32[]{:S(2)}, u32[]{:S(2)}) collective-permute-start(bf16[256,2048]{0,1:T(8,128)(2,1)} %get-tuple-element.530), channel_id=1, source_target_pairs={{0,8},{8,16},{16,24},{24,0},{1,9},{9,17},{17,25},{25,1},{2,10},{10... | collective-permute-start | bytes 3145736 | tf_op jit(solution)/shard_map/while/body/eval_jaxpr/ppermute | solution.py:18
  996.6 73.1 %collective-permute-start.2 = (bf16[256,2048]{0,1:T(8,128)(2,1)}, bf16[256,2048]{0,1:T(8,128)(2,1)}, u32[]{:S(2)}, u32[]{:S(2)}) collective-permute-start(bf16[256,2048]{0,1:T(8,128)(2,1)} %get-tuple-element.532), channel_id=1, source_target_pairs={{0,8},{8,16},{16,24},{24,0},{1,9},{9,17},{17,25},{25,1},{2,10},{10... | collective-permute-start | bytes 3145736 | tf_op jit(solution)/shard_map/while/body/eval_jaxpr/ppermute | solution.py:18
  997.4 91.9 %collective-permute-start.3 = (bf16[256,2048]{0,1:T(8,128)(2,1)}, bf16[256,2048]{0,1:T(8,128)(2,1)}, u32[]{:S(2)}, u32[]{:S(2)}) collective-permute-start(bf16[256,2048]{0,1:T(8,128)(2,1)} %get-tuple-element.533), channel_id=1, source_target_pairs={{0,8},{8,16},{16,24},{24,0},{1,9},{9,17},{17,25},{25,1},{2,10},{10... | collective-permute-start | bytes 3145736 | tf_op jit(solution)/shard_map/while/body/eval_jaxpr/ppermute | solution.py:18
  1025.7 22.5 %copy-start.23 = (bf16[256,32,64]{0,2,1:T(8,128)(2,1)S(1)}, bf16[256,32,64]{0,2,1:T(8,128)(2,1)}, u32[]{:S(2)}) copy-start(bf16[256,32,64]{0,2,1:T(8,128)(2,1)} %get-tuple-element.558) | copy-start | bytes 3145732 | tf_op jit(solution)/shard_map/while
  1053.5 19.0 copy-start
  1073.9 2.2 copy-start.1
  1092.0 28.1 %collective-permute-start.4 = (bf16[256,2048]{0,1:T(8,128)(2,1)}, bf16[256,2048]{0,1:T(8,128)(2,1)S(1)}, u32[]{:S(2)}, u32[]{:S(2)}) collective-permute-start(bf16[256,2048]{0,1:T(8,128)(2,1)} %get-tuple-element.321), channel_id=1, source_target_pairs={{0,8},{8,16},{16,24},{24,0},{1,9},{9,17},{17,25},{25,1},{2,10},{10... | collective-permute-start | bytes 3145736 | tf_op jit(solution)/shard_map/ppermute | solution.py:18
  1092.1 46.8 %collective-permute-start.5 = (bf16[256,2048]{0,1:T(8,128)(2,1)}, bf16[256,2048]{0,1:T(8,128)(2,1)S(1)}, u32[]{:S(2)}, u32[]{:S(2)}) collective-permute-start(bf16[256,2048]{0,1:T(8,128)(2,1)} %get-tuple-element.322), channel_id=1, source_target_pairs={{0,8},{8,16},{16,24},{24,0},{1,9},{9,17},{17,25},{25,1},{2,10},{10... | collective-permute-start | bytes 3145736 | tf_op jit(solution)/shard_map/ppermute | solution.py:18
  1092.1 28.4 %copy-start.30 = (f32[256,8]{0,1:T(8,128)S(1)}, f32[256,8]{0,1:T(8,128)}, u32[]{:S(2)}) copy-start(f32[256,8]{0,1:T(8,128)} %copy-done.29) | copy-start | bytes 24580
  1092.1 28.4 %copy-start.32 = (f32[256,8]{0,1:T(8,128)S(1)}, f32[256,8]{0,1:T(8,128)}, u32[]{:S(2)}) copy-start(f32[256,8]{0,1:T(8,128)} %copy-done.31) | copy-start | bytes 24580
  1120.5 19.4 copy-start.3
  1120.5 19.4 copy-start.17
  1120.5 19.3 copy-start.19
  1120.5 19.3 copy-start.26
  1120.5 19.3 copy-start.28
  1122.1 33.1 %copy-start.11 = (bf16[256,32,64]{0,2,1:T(8,128)(2,1)}, bf16[256,32,64]{0,2,1:T(8,128)(2,1)S(1)}, u32[]{:S(2)}) copy-start(bf16[256,32,64]{0,2,1:T(8,128)(2,1)S(1)} %get-tuple-element.429) | copy-start | bytes 3145732
  1155.3 919.6 %all-reduce.11.cloned.1.call-start = ((), (), s32[]{:S(2)}) async-start(), calls=%async_computation.14 | async-start | bytes 25690112 | tf_op jit(solution)/shard_map/psum | solution.py:339
  1645.8 13.1 copy-start.7
  1658.9 5.9 copy-start.10
  1664.8 12.3 copy-start.12
  1677.1 43.0 %copy-start.6 = (bf16[1,256,2048]{2,1,0:T(8,128)(2,1)S(1)}, bf16[1,256,2048]{2,1,0:T(8,128)(2,1)}, u32[]{:S(2)}) copy-start(bf16[1,256,2048]{2,1,0:T(8,128)(2,1)} %param.21) | copy-start | bytes 3145732
  2074.9 5.4 copy-start.21
  2080.3 2.6 copy-start.15
  2082.9 3.2 copy-start.14
  2086.1 3.2 copy-start.13
  (5 other events, 5.4 us)
Sparse Core Ops, SparseCore 0:
  9.9 128.0 all-gather.9
  139.8 116.4 all-gather.17
  258.2 116.4 all-gather.19
  376.5 116.4 all-gather.21
  494.7 54.3 all-gather.15
  550.6 80.7 all-gather.13
  632.9 79.0 all-gather.11
  715.9 532.1 all-reduce.8
  1252.0 71.2 reduce-scatter.5
  1326.8 145.8 reduce-scatter.7
  1476.3 156.8 reduce-scatter.3
  1637.3 437.5 all-reduce.10
where the time goes:
time: 2110 us; the launch traced here: 2100 us
  waiting for transfers between devices  1650 us (78%)
  matrix products  263 us (12%)
  other arithmetic  60.7 us (3%)
  blocking collectives  46.8 us (2%)
  local copies, waits for them, and re-layouts  43.4 us (2%)
    psum x1, waiting for transfers between devices, body(): lax.psum(grad_qkv.astype(jnp.bfloat16), 'ctx').astype(jnp.float32)  351 us
    ppermute x14, waiting for transfers between devices, from_behind(): return lax.ppermute(value, axis, pairs)  264 us
    reduce_scatter x1, waiting for transfers between devices, body(): lax.psum_scatter(full_qkv.astype(jnp.bfloat16), 'fsdp', scatter_dimension...  161 us
    reduce_scatter x1, waiting for transfers between devices, body(): lax.psum_scatter(lax.dot_general(part, grad_low, contract_rows, preferred...  149 us
    all_gather x1, waiting for transfers between devices, body(): lax.all_gather(shards[2], 'fsdp', axis=0, tiled=True)  107 us
    all_gather x1, waiting for transfers between devices, body(): lax.all_gather(shards[5], 'fsdp', axis=0, tiled=True)  105 us
    all_gather x1, waiting for transfers between devices, body(): lax.all_gather(shards[4], 'fsdp', axis=0, tiled=True)  102 us
    all_gather x1, waiting for transfers between devices, body(): lax.all_gather(shards[6], 'fsdp', axis=0, tiled=True)  96.9 us
  transfers between devices with their start and end apart: 26, of which 26 were waited for; matrix products, arithmetic and copies ran while one was open for 16% of the time, Pallas kernels for 0%

commit v1 on v0

v1 whole, which is shorter than its diff:
```python
import functools

import jax
import jax.numpy as jnp
from jax import lax
from jax.experimental import pallas as pl
from jax.experimental.pallas import tpu as pltpu
from jax.sharding import PartitionSpec as P

H = 32
HD = 64
ROT = 16
EPS = 1e-05
NEG = -1e30
CHUNK = 256

BF = jnp.bfloat16
F32 = jnp.float32


def xor_send(value, mask):
    count = lax.axis_size("fsdp")
    return lax.ppermute(value, "fsdp", [(i, i ^ mask) for i in range(count)])


def ring_send(value, steps):
    count = lax.axis_size("ctx")
    return lax.ppermute(value, "ctx", [(i, (i + steps) % count) for i in range(count)])


def after(value, *done):
    return lax.optimization_barrier((value,) + done)[0]


def dot(a, b, dims, out=F32):
    return lax.dot_general(a, b, (dims, ((), ())), preferred_element_type=F32).astype(out)


def gather_rows(piece):
    count = lax.axis_size("fsdp")
    chips = count // 2
    me = lax.axis_index("fsdp")
    chip, core = me // 2, me % 2
    parts = [piece] + [xor_send(piece, 2 * m) for m in range(1, chips)]
    others = [xor_send(p, 1) for p in parts]
    whole = jnp.zeros((count,) + piece.shape, piece.dtype)
    for m in range(chips):
        at = 2 * (chip ^ m)
        whole = lax.dynamic_update_index_in_dim(whole, parts[m], at + core, 0)
        whole = lax.dynamic_update_index_in_dim(whole, others[m], at + 1 - core, 0)
    return whole.reshape(count * piece.shape[0], piece.shape[1]), parts[-1]


def scatter_rows(grad):
    count = lax.axis_size("fsdp")
    chips = count // 2
    me = lax.axis_index("fsdp")
    chip, core = me // 2, me % 2
    rows = grad.shape[0] // count
    split = grad.reshape(chips, 2, rows, grad.shape[1])
    theirs = xor_send(lax.dynamic_index_in_dim(split, 1 - core, 1, False), 1)
    pair = lax.dynamic_index_in_dim(split, core, 1, False).astype(F32) + theirs.astype(F32)
    pair = pair.astype(BF)
    total = lax.dynamic_index_in_dim(pair, chip, 0, False).astype(F32)
    for m in range(1, chips):
        part = lax.dynamic_index_in_dim(pair, chip ^ m, 0, False)
        total = total + xor_send(part, 2 * m).astype(F32)
    return total.astype(BF)


def gather_ctx(piece):
    count = lax.axis_size("ctx")
    me = lax.axis_index("ctx")
    whole = jnp.zeros((count,) + piece.shape, piece.dtype)
    whole = lax.dynamic_update_index_in_dim(whole, piece, me, 0)
    for k in range(1, count):
        part = ring_send(piece, k)
        whole = lax.dynamic_update_index_in_dim(whole, part, (me - k) % count, 0)
    return whole


def line_scatter(blocks):
    count = lax.axis_size("ctx")
    me = lax.axis_index("ctx")
    down = up = None
    for t in range(1, count):
        to_down = blocks(jnp.clip(t + me - count, 0, count - 1))
        to_up = blocks(jnp.clip(count - 1 - (t + (count - 1 - me) - count), 0, count - 1))
        if down is not None:
            to_down = to_down + down.astype(F32)
            to_up = to_up + up.astype(F32)
        pairs = [(i, i - 1) for i in range(count - t, count)]
        down = lax.ppermute(to_down.astype(BF), "ctx", pairs)
        up = lax.ppermute(to_up.astype(BF), "ctx", [(count - 1 - i, count - 1 - j) for i, j in pairs])
    return blocks(me) + down.astype(F32) + up.astype(F32)


def turn(x, cos, first, second):
    width = x.shape[1]
    half = ROT // 2
    return x * cos + pltpu.roll(x, width - half, 1) * first + pltpu.roll(x, half, 1) * second


def contract(a, b, dims):
    return lax.dot_general(a, b, (dims, ((), ())), preferred_element_type=F32)


def attend_kernel(mq, mk, mv, cos, first, second, q_out, k_out, v_out, att_out, lse_out):
    length = mq.shape[0]
    scale = HD ** (-0.5)
    q_out[...] = (turn(mq[...], cos[...], first[...], second[...]).astype(BF).astype(F32) * scale).astype(BF)
    k_out[...] = turn(mk[...], cos[...], first[...], second[...]).astype(BF)
    v_out[...] = mv[...].astype(BF)
    row = lax.broadcasted_iota(jnp.int32, (CHUNK, CHUNK), 0)
    col = lax.broadcasted_iota(jnp.int32, (CHUNK, CHUNK), 1)
    for c in range(length // CHUNK):
        lo, hi = c * CHUNK, (c + 1) * CHUNK
        for h in range(2):
            lanes = slice(h * HD, (h + 1) * HD)
            q = q_out[lo:hi, lanes]
            s = contract(q, k_out[lo:hi, lanes], ((1,), (1,)))
            s = jnp.where(col <= row, s, NEG)
            if c:
                s = jnp.concatenate([contract(q, k_out[:lo, lanes], ((1,), (1,))), s], axis=1)
            top = jnp.max(s, axis=1, keepdims=True)
            p = jnp.exp(s - top)
            total = jnp.sum(p, axis=1, keepdims=True)
            o = contract(p.astype(BF), v_out[:hi, lanes], ((1,), (0,)))
            att_out[lo:hi, lanes] = o / total
            lse_out[lo:hi, lanes] = jnp.broadcast_to(top + jnp.log(total), (CHUNK, HD))


def attend(mixed, tables, heads):
    length = mixed.shape[0]
    pairs = heads // 2
    block = lambda at: pl.BlockSpec((length, 2 * HD), lambda h, at=at: (0, at + h))
    table = pl.BlockSpec((length, 2 * HD), lambda h: (0, 0))
    width = heads * HD
    return pl.pallas_call(
        attend_kernel,
        grid=(pairs,),
        in_specs=[block(0), block(pairs), block(2 * pairs), table, table, table],
        out_specs=[block(0)] * 5,
        out_shape=[jax.ShapeDtypeStruct((length, width), BF)] * 3
        + [jax.ShapeDtypeStruct((length, width), F32)] * 2,
        compiler_params=pltpu.CompilerParams(vmem_limit_bytes=40 * 2**20),
        cost_estimate=pl.CostEstimate(
            flops=16 * heads * length * length * HD // 2,
            bytes_accessed=26 * length * width,
            transcendentals=heads * length * length // 2,
        ),
        name="attend",
    )(mixed, mixed, mixed, *tables)


def attend_back_kernel(q_in, k_in, v_in, do_in, att, lse, cos, first, second, dq_out, dk_out, dv_out, dk, dv):
    length = q_in.shape[0]
    scale = HD ** (-0.5)
    row = lax.broadcasted_iota(jnp.int32, (CHUNK, CHUNK), 0)
    col = lax.broadcasted_iota(jnp.int32, (CHUNK, CHUNK), 1)
    dk[...] = jnp.zeros_like(dk)
    dv[...] = jnp.zeros_like(dv)
    for c in range(length // CHUNK):
        lo, hi = c * CHUNK, (c + 1) * CHUNK
        dqs = []
        for h in range(2):
            lanes = slice(h * HD, (h + 1) * HD)
            q, do = q_in[lo:hi, lanes], do_in[lo:hi, lanes]
            delta = jnp.sum(do.astype(F32) * att[lo:hi, lanes], axis=1, keepdims=True)
            s = contract(q, k_in[lo:hi, lanes], ((1,), (1,)))
            s = jnp.where(col <= row, s, NEG)
            if c:
                s = jnp.concatenate([contract(q, k_in[:lo, lanes], ((1,), (1,))), s], axis=1)
            p = jnp.exp(s - lse[lo:hi, h * HD : h * HD + 1])
            dp = contract(do, v_in[:hi, lanes], ((1,), (1,)))
            ds = (p * (dp - delta)).astype(BF)
            dqs.append(contract(ds, k_in[:hi, lanes], ((1,), (0,))) * scale)
            dk[:hi, lanes] += contract(ds, q, ((0,), (0,)))
            dv[:hi, lanes] += contract(p.astype(BF), do, ((0,), (0,)))
        dq = jnp.concatenate(dqs, axis=1)
        dq_out[lo:hi, :] = turn(dq, cos[lo:hi, :], -first[lo:hi, :], -second[lo:hi, :]).astype(BF)
    dk_out[...] = turn(dk[...], cos[...], -first[...], -second[...]).astype(BF)
    dv_out[...] = dv[...].astype(BF)


def attend_back(q, k, v, d_attended, attended, lse, tables, heads):
    length, width = q.shape
    block = pl.BlockSpec((length, 2 * HD), lambda h: (0, h))
    table = pl.BlockSpec((length, 2 * HD), lambda h: (0, 0))
    return pl.pallas_call(
        attend_back_kernel,
        grid=(heads // 2,),
        in_specs=[block] * 6 + [table] * 3,
        out_specs=[block] * 3,
        out_shape=[jax.ShapeDtypeStruct((length, width), BF)] * 3,
        scratch_shapes=[pltpu.VMEM((length, 2 * HD), F32)] * 2,
        compiler_params=pltpu.CompilerParams(vmem_limit_bytes=40 * 2**20),
        cost_estimate=pl.CostEstimate(
            flops=40 * heads * length * length * HD // 2,
            bytes_accessed=22 * length * width,
            transcendentals=heads * length * length // 2,
        ),
        name="attend_back",
    )(q, k, v, d_attended, attended, lse, *tables)


def rotation_tables(length):
    half = ROT // 2
    inverse = 10000.0 ** (-jnp.arange(half, dtype=F32) / half)
    grid = jnp.arange(length, dtype=jnp.int32).astype(F32)[:, None] * inverse[None, :]
    cos, sin = jnp.cos(grid), jnp.sin(grid)
    zero = jnp.zeros((length, half), F32)
    rest = jnp.zeros((length, HD - ROT), F32)
    tables = (
        jnp.concatenate([cos, cos, rest + 1.0], axis=1),
        jnp.concatenate([-sin, zero, rest], axis=1),
        jnp.concatenate([zero, sin, rest], axis=1),
    )
    return tuple(jnp.tile(t, (1, 2)) for t in tables)


def body(tokens, block_order, ln_gain, ln_bias, w_qkv, w_out, w_gate, w_up, w_down, cotangent):
    rows, width = tokens.shape[1], tokens.shape[2]
    count = lax.axis_size("ctx")
    shards = lax.axis_size("fsdp")
    place = lax.axis_index("ctx")
    length = rows * count
    order = block_order[0]
    shard_rows = w_qkv.shape[0]
    ff_shard = w_down.shape[0]
    ff_part = ff_shard // count
    own_heads = H // count
    spread = (w_out.shape[0] // HD) % count == 0
    groups = shards if spread else 1
    head_cols = own_heads * HD // groups

    def my_cols(w, outer, group, part):
        w = w.reshape(w.shape[0], outer, group, count, part)
        return lax.dynamic_index_in_dim(w, place, 3, False).reshape(w.shape[0], outer * group * part)

    def all_cols(piece, outer, group, part):
        whole = gather_ctx(piece).reshape(count, piece.shape[0], outer, group, part)
        return whole.transpose(1, 2, 3, 0, 4).reshape(piece.shape[0], -1).astype(F32)

    def assemble(block, ready=None):
        whole = jnp.zeros((length, width), block.dtype)
        whole = lax.dynamic_update_slice_in_dim(whole, block, order[place] * rows, 0)
        last = None
        for k in range(1, count):
            last = ring_send(block, k)
            source = (place - k) % count
            whole = lax.dynamic_update_slice_in_dim(whole, last, order[source] * rows, 0)
        return whole, last

    gain = lax.all_gather(ln_gain, "fsdp", axis=0, tiled=True).astype(F32)
    bias = lax.all_gather(ln_bias, "fsdp", axis=0, tiled=True).astype(F32)
    tables = rotation_tables(length)

    block = tokens[0]
    x_all, arrived = assemble(block)
    grad_block = cotangent[0]
    cot_all, _ = assemble(after(grad_block, arrived))

    inner = jnp.concatenate(
        [my_cols(w_gate, 1, shards, ff_part), my_cols(w_up, 1, shards, ff_part)], axis=1
    )
    w_inner, sent = gather_rows(inner)
    w_heads, sent = gather_rows(after(my_cols(w_qkv, 3, groups, head_cols), sent))
    down = lax.dynamic_slice_in_dim(w_down, place * ff_part, ff_part, 0)
    w_hidden, sent = gather_rows(after(down, sent))
    if spread:
        part = w_out.shape[0] // count
        attn = lax.dynamic_slice_in_dim(w_out, place * part, part, 0)
        w_attn, sent = gather_rows(after(attn, sent))
    else:
        w_attn = lax.all_gather(after(w_out, sent), "fsdp", axis=0, tiled=True)
        w_attn = lax.dynamic_slice_in_dim(w_attn, place * own_heads * HD, own_heads * HD, 0)

    xf = x_all.astype(F32)
    average = jnp.mean(xf, axis=-1, keepdims=True)
    centered = xf - average
    variance = jnp.mean(centered * centered, axis=-1, keepdims=True)
    inv_std = lax.rsqrt(variance + EPS)
    x_hat = centered * inv_std
    normed = (x_hat * gain + bias).astype(BF)

    across = ((1,), (0,))
    over_tokens = ((0,), (0,))
    back = ((1,), (1,))
    ff_cols = shards * ff_part
    gate_value = dot(normed, w_inner[:, :ff_cols], across)
    up_value = dot(normed, w_inner[:, ff_cols:], across)
    sigmoid_gate = jax.nn.sigmoid(gate_value)
    hidden = (gate_value * sigmoid_gate * up_value).astype(BF)
    mixed = dot(normed, w_heads, across)
    q, k, v, attended, lse = attend(mixed, tables, own_heads)
    attended_low = attended.astype(BF)

    branch = dot(attended_low, w_attn, across) + dot(hidden, w_hidden, across)
    out = line_scatter(lambda j: lax.dynamic_slice_in_dim(branch, order[j] * rows, rows, 0))
    out = (block.astype(F32) + out).astype(BF)[None]

    d_hidden = dot(cot_all, w_hidden, back)
    grad_down = scatter_rows(dot(hidden, cot_all, over_tokens, BF))
    d_gate_act = (
        d_hidden * up_value * sigmoid_gate * (1.0 + gate_value * (1.0 - sigmoid_gate))
    ).astype(BF)
    d_up_act = (d_hidden * gate_value * sigmoid_gate).astype(BF)
    d_inner = jnp.concatenate([d_gate_act, d_up_act], axis=1)
    d_attended = dot(cot_all, w_attn, back, BF)
    d_mixed = attend_back(q, k, v, d_attended, attended, lse, tables, own_heads)
    d_mixed = jnp.concatenate(d_mixed, axis=1)
    grad_inner = scatter_rows(dot(normed, d_inner, over_tokens, BF))
    grad_attn = dot(attended_low, cot_all, over_tokens, BF)
    grad_heads = scatter_rows(dot(normed, d_mixed, over_tokens, BF))

    d_normed = dot(d_inner, w_inner, back) + dot(d_mixed, w_heads, back)
    small = jnp.stack([jnp.sum(d_normed * x_hat, axis=0), jnp.sum(d_normed, axis=0)])
    small = lax.psum(small, ("ctx", "fsdp"))
    small = lax.dynamic_slice_in_dim(small, lax.axis_index("fsdp") * shard_rows, shard_rows, 1)
    d_own = line_scatter(lambda j: lax.dynamic_slice_in_dim(d_normed, order[j] * rows, rows, 0))
    own = block.astype(F32)
    own_average = jnp.mean(own, axis=-1, keepdims=True)
    own = own - own_average
    own_std = lax.rsqrt(jnp.mean(own * own, axis=-1, keepdims=True) + EPS)
    own = own * own_std
    scaled = d_own * gain
    d_input = own_std * (
        scaled
        - jnp.mean(scaled, axis=-1, keepdims=True)
        - own * jnp.mean(scaled * own, axis=-1, keepdims=True)
    )
    grad_in = (grad_block.astype(F32) + d_input)[None]

    down_all = gather_ctx(grad_down).reshape(ff_shard, width).astype(F32)
    if spread:
        attn_all = gather_ctx(scatter_rows(grad_attn)).reshape(w_out.shape).astype(F32)
    else:
        full = jnp.zeros((H * HD, width), BF)
        full = lax.dynamic_update_slice_in_dim(full, grad_attn, place * own_heads * HD, 0)
        full = lax.psum_scatter(full, "fsdp", scatter_dimension=0, tiled=True)
        attn_all = lax.psum(full, "ctx").astype(F32)
    heads_all = all_cols(grad_heads, 3, groups, head_cols)
    inner_all = gather_ctx(grad_inner).reshape(count, shard_rows, 2, shards, ff_part)
    inner_all = inner_all.transpose(2, 1, 3, 0, 4).reshape(2, shard_rows, -1).astype(F32)
    return (
        out,
        grad_in,
        small[0],
        small[1],
        heads_all,
        attn_all,
        inner_all[0],
        inner_all[1],
        down_all,
    )


def solution(mesh):
    whole, once = P("fsdp", "ctx", None), P("fsdp", None)
    return jax.shard_map(
        body,
        mesh=mesh,
        in_specs=(whole, once, P("fsdp"), P("fsdp")) + (once,) * 5 + (whole,),
        out_specs=(whole, whole, P("fsdp"), P("fsdp")) + (once,) * 5,
        check_vma=False,
    )
```

time: 2110 us -> 1080 us (0.51)
  the two profiles are of different devices: /device:TPU:0 before, /device:TPU:11 now
where the time goes in v1:
time: 1080 us; the launch traced here: 1070 us
  waiting for transfers between devices  432 us (40%)
  local copies, waits for them, and re-layouts  246 us (23%)
  matrix products  134 us (12%)
  starting transfers between devices  76.4 us (7%)
  other arithmetic  60.3 us (6%)
  blocking collectives  58.1 us (5%)
  Pallas kernels  53 us (5%)
    ppermute x18, waiting for transfers between devices, ring_send(): lax.ppermute(value, 'ctx', [(i, (i + steps) % count) for i in range(count)])  271 us
    dot_general x13, matrix products, dot(): lax.dot_general(a, b, (dims, ((), ())), preferred_element_type=F32)  134 us
    ppermute x44, waiting for transfers between devices, xor_send(): return lax.ppermute(value, 'fsdp', [(i, i ^ mask) for i in range(count)])  94.6 us
    ppermute x6, waiting for transfers between devices, line_scatter(): down = lax.ppermute(to_down.astype(BF), 'ctx', pairs)  47.7 us
    unnamed x112, local copies, waits for them, and re-layouts  47.2 us
    psum x1, blocking collectives, body(): small = lax.psum(small, ('ctx', 'fsdp'))  41.5 us
    pallas_call x1, Pallas kernels, attend_back(): pl.pallas_call(attend_back_kernel, grid=(heads // 2,), in_specs=[block] *...  33.6 us
    ppermute x44, starting transfers between devices, xor_send(): return lax.ppermute(value, 'fsdp', [(i, i ^ mask) for i in range(count)])  31.7 us
  transfers between devices with their start and end apart: 74, of which 25 were waited for; matrix products, arithmetic and copies ran while one was open for 37% of the time, Pallas kernels for 5%

profile of v1, /device:TPU:11, one launch (start us, length us, event | category | flops | bytes accessed | tf_op | source)
XLA Modules:
  0.0 1068.3 jit_solution(10995127384491180597)
XLA Ops:
  4.5 4.5 copy.75
  9.0 4.5 copy.74
  21.8 4.6 copy.73
  31.0 4.9 broadcast_in_dim.219
  47.8 8.7 all-gather
  56.5 7.9 all-gather.1
  75.8 18.6 %collective-permute-done.2 = bf16[256,2048]{1,0:T(8,128)(2,1)} collective-permute-done((bf16[256,2048]{1,0:T(8,128)(2,1)}, bf16[256,2048]{1,0:T(8,128)(2,1)}, u32[]{:S(2)}, u32[]{:S(2)}) %collective-permute-start.2) | collective-permute-done | bytes 1048608 | tf_op jit(solution)/shard_map/ppermute | solution.py:28
  111.8 15.6 %collective-permute-done.20 = bf16[256,2816]{0,1:T(8,128)(2,1)} collective-permute-done((bf16[256,2816]{0,1:T(8,128)(2,1)}, bf16[256,2816]{0,1:T(8,128)(2,1)}, u32[]{:S(2)}, u32[]{:S(2)}) %collective-permute-start.20) | collective-permute-done | bytes 1441824 | tf_op jit(solution)/shard_map/ppermute | solution.py:23
  133.2 53.6 %collective-permute-done.38 = bf16[256,2048]{1,0:T(8,128)(2,1)} collective-permute-done((bf16[256,2048]{1,0:T(8,128)(2,1)}, bf16[256,2048]{1,0:T(8,128)(2,1)}, u32[]{:S(2)}, u32[]{:S(2)}) %collective-permute-start.38) | collective-permute-done | bytes 1048608 | tf_op jit(solution)/shard_map/ppermute | solution.py:28
  219.8 3.3 broadcast_in_dim.228
  242.3 11.3 %fusion.10 = f32[1024,1408]{1,0:T(8,128)} fusion(bf16[2048,2816]{1,0:T(8,128)(2,1)} %bitcast.232, bf16[1024,2048]{1,0:T(8,128)(2,1)S(1)} %copy-done.8, f32[2048]{0:T(1024)S(1)} %bitcast.259, f32[2048]{0:T(1024)S(1)} %bitcast.253, f32[1024]{0:T(1024)S(1)} %add_rsqrt_fusion, f32[1024]{0:T(1024)S(1)} %broadcast_multiply_fusion), kind=kOutput, calls=%fused_computation.19 | convolution fusion | flops 5918162944 | bytes 15753216 | tf_op jit(solution)/shard_map/dot_general | solution.py:36
  277.9 11.7 %fusion.50.mq.mk.mv = f32[1024,1536]{1,0:T(8,128)} fusion(bf16[2048,1536]{1,0:T(8,128)(2,1)} %bitcast.21, bf16[1024,2048]{1,0:T(8,128)(2,1)S(1)} %copy-done.9, f32[2048]{0:T(1024)S(1)} %bitcast.260, f32[2048]{0:T(1024)S(1)} %bitcast.254, f32[1024]{0:T(1024)S(1)} %add_rsqrt_fusion, f32[1024]{0:T(1024)S(1)} %broadcast_multiply_fusion), kind=kOutput, calls=%fused_computation.196 | convolution fusion | flops 6455033856 | bytes 16801792 | tf_op jit(solution)/shard_map/dot_general | solution.py:36
  289.6 19.4 %attend.1 = (bf16[1024,512]{1,0:T(8,128)(2,1)S(1)}, bf16[1024,512]{1,0:T(8,128)(2,1)S(1)}, bf16[1024,512]{1,0:T(8,128)(2,1)S(1)}, f32[1024,512]{1,0:T(8,128)S(1)}, f32[1024,512]{1,0:T(8,128)S(1)}) custom-call(f32[1024,1536]{1,0:T(8,128)} %fusion.50.mq.mk.mv, f32[1024,1536]{1,0:T(8,128)} %fusion.50.mq.mk.mv, f32[1024,1536]{1,0:T(8,128)} %fusion.50.mq.mk.mv, ...), custom_call_target="tpu_custom_call" | custom-call | flops 4294967296 | bytes 13631488 | tf_op jit(solution)/shard_map/attend/pallas_call | solution.py:139
  323.9 33.6 %attend_back.1 = (bf16[1024,512]{1,0:T(8,128)(2,1)S(1)}, bf16[1024,512]{1,0:T(8,128)(2,1)S(1)}, bf16[1024,512]{1,0:T(8,128)(2,1)S(1)}) custom-call(bf16[1024,512]{1,0:T(8,128)(2,1)S(1)} %get-tuple-element.26.q_in, bf16[1024,512]{1,0:T(8,128)(2,1)S(1)} %get-tuple-element.27.k_in, bf16[1024,512]{1,0:T(8,128)(2,1)S(1)} %get-tuple-element.28.v_in, ...), custom_call_target="tpu_custom_call" | custom-call | flops 10737418240 | bytes 11534336 | tf_op jit(solution)/shard_map/attend_back/pallas_call | solution.py:190
  357.8 7.6 convolution_convert_fusion.2
  365.4 11.0 %fusion.61 = f32[1024,2048]{1,0:T(8,128)} fusion(bf16[1024,1536]{1,0:T(8,128)(2,1)S(1)} %constant_dynamic-update-slice_fusion.24, bf16[2048,1536]{1,0:T(8,128)(2,1)} %bitcast.21), kind=kOutput, calls=%fused_computation.202 | convolution fusion | flops 6442450944 | bytes 17825792 | tf_op jit(solution)/shard_map/dot_general | solution.py:36
  378.5 4.7 copy.99
  396.7 10.6 fusion.60
  407.3 13.8 %multiply_convert_fusion.1 = (bf16[1024,1408]{1,0:T(8,128)(2,1)S(1)}, bf16[1024,1408]{1,0:T(8,128)(2,1)S(1)}, bf16[1024,1408]{1,0:T(8,128)(2,1)S(1)}) fusion(f32[1024,1408]{1,0:T(8,128)} %fusion.60, f32[1024,1408]{1,0:T(8,128)} %fusion.10, bf16[2048,2816]{1,0:T(8,128)(2,1)} %bitcast.233, bf16[1024,2048]{1,0:T(8,128)(2,1)S(1)} %copy-done.10, ...), kind=kOutput, calls=%fused_computation.27 | convolution fusion | flops 5941231616 | bytes 30171136 | tf_op jit(solution)/shard_map/dot_general | solution.py:36
  421.1 11.8 %fusion.59 = f32[1024,2048]{1,0:T(8,128)} fusion(bf16[1024,1408]{1,0:T(8,128)(2,1)S(1)} %get-tuple-element.78, bf16[1408,2048]{1,0:T(8,128)(2,1)} %bitcast.51), kind=kOutput, calls=%fused_computation.200 | convolution fusion | flops 5905580032 | bytes 17039360 | tf_op jit(solution)/shard_map/dot_general | solution.py:36
  433.0 8.2 convolution_convert_fusion.1
  441.2 17.5 %convolution_convert_fusion = bf16[2048,2816]{1,0:T(8,128)(2,1)} fusion(bf16[1024,1408]{1,0:T(8,128)(2,1)S(1)} %get-tuple-element.79, bf16[1024,1408]{1,0:T(8,128)(2,1)S(1)} %get-tuple-element.77, bf16[1024,2048]{1,0:T(8,128)(2,1)S(1)} %copy-done.10, f32[2048]{0:T(1024)S(1)} %bitcast.263, f32[2048]{0:T(1024)S(1)} %bitcast.257, f32[1024]{0:T(1024)S(1)} %add_rsqrt_fusion, ...), kind=kOutput, calls=%fused_computation.3 | convolution fusion | flops 11841044480 | bytes 21520384 | tf_op jit(solution)/shard_map/dot_general | solution.py:36
  458.7 20.1 %fusion.7 = (f32[2048]{0:T(1024)S(1)}, f32[2048]{0:T(1024)S(1)}, f32[1024,2048]{1,0:T(8,128)}) fusion(bf16[1024,2048]{1,0:T(8,128)(2,1)} %copy-done.7, f32[1024]{0:T(1024)S(1)} %add_rsqrt_fusion, f32[1024]{0:T(1024)S(1)} %broadcast_multiply_fusion, f32[1024,2048]{1,0:T(8,128)} %fusion.61, bf16[2048,2816]{1,0:T(8,128)(2,1)} %bitcast.234, ...), kind=kOutput, calls=%fused_computation.12 | convolution fusion | flops 11837370368 | bytes 38297600 | tf_op jit(solution)/shard_map/dot_general | solution.py:36
  478.8 3.5 dynamic-slice_convert_fusion.1
  484.3 9.5 constant_dynamic-slice_fusion.2
  493.8 3.9 dynamic-slice_bitcast_fusion
  497.8 5.9 convolution_add_fusion.1
  510.5 4.4 collective-permute-done.56
  516.2 4.8 collective-permute-done.55
  523.7 8.3 copy.102
  532.0 8.3 copy.109
  540.3 41.5 %psum.7 = f32[2,2048]{1,0:T(2,128)S(1)} all-reduce(f32[2,2048]{1,0:T(2,128)S(1)} %pad_maximum_fusion.4), channel_id=1, replica_groups=mesh['ctx'=4,'fsdp'=8] {'ctx','fsdp'}, use_global_device_ids=true, to_apply=%region_8.9 | all-reduce | flops 4096 | bytes 32768 | tf_op jit(solution)/shard_map/psum | solution.py:319
  585.1 11.4 %collective-permute-done.58 = bf16[64,2048]{1,0:T(8,128)(2,1)S(1)} collective-permute-done((bf16[64,2048]{1,0:T(8,128)(2,1)}, bf16[64,2048]{1,0:T(8,128)(2,1)S(1)}, u32[]{:S(2)}, u32[]{:S(2)}) %collective-permute-start.58) | collective-permute-done | bytes 262176 | tf_op jit(solution)/shard_map/ppermute | solution.py:28
  601.6 3.8 collective-permute-done.59
  613.4 18.4 %collective-permute-done.41 = bf16[256,2048]{1,0:T(8,128)(2,1)S(1)} collective-permute-done((bf16[256,2048]{1,0:T(8,128)(2,1)S(1)}, bf16[256,2048]{1,0:T(8,128)(2,1)S(1)}, u32[]{:S(2)}, u32[]{:S(2)}) %collective-permute-start.41) | collective-permute-done | bytes 1048608 | tf_op jit(solution)/shard_map/ppermute | solution.py:93
  634.2 3.4 add_convert_fusion.2
  637.6 4.5 collective-permute-start.44
  642.1 12.3 %collective-permute-done.32 = bf16[256,2048]{1,0:T(8,128)(2,1)S(1)} collective-permute-done((bf16[256,2048]{1,0:T(8,128)(2,1)S(1)}, bf16[256,2048]{1,0:T(8,128)(2,1)S(1)}, u32[]{:S(2)}, u32[]{:S(2)}) %collective-permute-start.32) | collective-permute-done | bytes 1048608 | tf_op jit(solution)/shard_map/ppermute | solution.py:93
  656.1 4.5 collective-permute-start.35
  670.1 16.9 %collective-permute-done.35 = bf16[256,2048]{1,0:T(8,128)(2,1)S(1)} collective-permute-done((bf16[256,2048]{1,0:T(8,128)(2,1)}, bf16[256,2048]{1,0:T(8,128)(2,1)S(1)}, u32[]{:S(2)}, u32[]{:S(2)}) %collective-permute-start.35) | collective-permute-done | bytes 1048608 | tf_op jit(solution)/shard_map/ppermute | solution.py:94
  688.6 11.5 %collective-permute-done.69 = bf16[176,2048]{1,0:T(8,128)(2,1)} collective-permute-done((bf16[176,2048]{1,0:T(8,128)(2,1)}, bf16[176,2048]{1,0:T(8,128)(2,1)}, u32[]{:S(2)}, u32[]{:S(2)}) %collective-permute-start.69) | collective-permute-done | bytes 720928 | tf_op jit(solution)/shard_map/ppermute | solution.py:23
  702.4 10.6 collective-permute-done.49
  719.5 12.3 %collective-permute-done.48 = bf16[256,1536]{0,1:T(8,128)(2,1)S(1)} collective-permute-done((bf16[256,1536]{0,1:T(8,128)(2,1)S(1)}, bf16[256,1536]{0,1:T(8,128)(2,1)S(1)}, u32[]{:S(2)}, u32[]{:S(2)}) %collective-permute-start.48) | collective-permute-done | bytes 786464 | tf_op jit(solution)/shard_map/ppermute | solution.py:23
  733.7 3.4 collective-permute-start.36
  741.8 17.0 %collective-permute-done.33 = bf16[256,2048]{1,0:T(8,128)(2,1)S(1)} collective-permute-done((bf16[256,2048]{1,0:T(8,128)(2,1)S(1)}, bf16[256,2048]{1,0:T(8,128)(2,1)S(1)}, u32[]{:S(2)}, u32[]{:S(2)}) %collective-permute-start.33) | collective-permute-done | bytes 1048608 | tf_op jit(solution)/shard_map/ppermute | solution.py:93
  761.5 4.2 fusion.26
  765.7 10.7 collective-permute-done.71
  777.3 43.8 %collective-permute-done.72 = bf16[176,2048]{1,0:T(8,128)(2,1)} collective-permute-done((bf16[176,2048]{1,0:T(8,128)(2,1)S(1)}, bf16[176,2048]{1,0:T(8,128)(2,1)}, u32[]{:S(2)}, u32[]{:S(2)}) %collective-permute-start.72) | collective-permute-done | bytes 720928 | tf_op jit(solution)/shard_map/ppermute | solution.py:28
  823.2 6.8 fusion
  833.7 19.8 %collective-permute-done.73 = bf16[176,2048]{1,0:T(8,128)(2,1)} collective-permute-done((bf16[176,2048]{1,0:T(8,128)(2,1)S(1)}, bf16[176,2048]{1,0:T(8,128)(2,1)}, u32[]{:S(2)}, u32[]{:S(2)}) %collective-permute-start.73) | collective-permute-done | bytes 720928 | tf_op jit(solution)/shard_map/ppermute | solution.py:28
  855.6 5.1 bitcast_convert_fusion
  864.8 33.1 %collective-permute-done.62 = bf16[256,2816]{0,1:T(8,128)(2,1)S(1)} collective-permute-done((bf16[256,2816]{0,1:T(8,128)(2,1)S(1)}, bf16[256,2816]{0,1:T(8,128)(2,1)S(1)}, u32[]{:S(2)}, u32[]{:S(2)}) %collective-permute-start.62) | collective-permute-done | bytes 1441824 | tf_op jit(solution)/shard_map/ppermute | solution.py:23
  898.2 3.4 bitcast_dynamic-update-slice_fusion.3
  903.4 3.3 collective-permute-start.65
  907.7 3.4 copy.100
  911.0 6.6 copy.105
  918.4 16.1 %collective-permute-done.64 = bf16[256,2816]{0,1:T(8,128)(2,1)} collective-permute-done((bf16[256,2816]{0,1:T(8,128)(2,1)}, bf16[256,2816]{0,1:T(8,128)(2,1)}, u32[]{:S(2)}, u32[]{:S(2)}) %collective-permute-start.64) | collective-permute-done | bytes 1441824 | tf_op jit(solution)/shard_map/ppermute | solution.py:28
  937.2 85.3 %collective-permute-done.65 = bf16[256,2816]{0,1:T(8,128)(2,1)} collective-permute-done((bf16[256,2816]{0,1:T(8,128)(2,1)}, bf16[256,2816]{0,1:T(8,128)(2,1)}, u32[]{:S(2)}, u32[]{:S(2)}) %collective-permute-start.65) | collective-permute-done | bytes 1441824 | tf_op jit(solution)/shard_map/ppermute | solution.py:28
  1025.0 4.8 collective-permute-done.66
  1031.0 8.4 convert_bitcast_fusion
  1039.4 7.6 fusion.57
  1049.9 6.2 copy.106
  1056.1 5.6 copy.104
  1061.7 6.4 copy.107
  (368 shorter events, 251.6 us)
Async XLA Ops:
  0.7 94.0 %collective-permute-start = (bf16[256,2048]{1,0:T(8,128)(2,1)}, bf16[256,2048]{1,0:T(8,128)(2,1)}, u32[]{:S(2)}, u32[]{:S(2)}) collective-permute-start(bf16[256,2048]{1,0:T(8,128)(2,1)} %bitcast.219), channel_id=1, source_target_pairs={{0,8},{8,16},{16,24},{24,0},{1,9},{9,17},{17,25},{25,1},{2,10},{10... | collective-permute-start | bytes 3145736 | tf_op jit(solution)/shard_map/ppermute | solution.py:28
  2.0 95.3 %collective-permute-start.1 = (bf16[256,2048]{1,0:T(8,128)(2,1)}, bf16[256,2048]{1,0:T(8,128)(2,1)}, u32[]{:S(2)}, u32[]{:S(2)}) collective-permute-start(bf16[256,2048]{1,0:T(8,128)(2,1)} %bitcast.220), channel_id=1, source_target_pairs={{0,16},{8,24},{16,0},{24,8},{1,17},{9,25},{17,1},{25,9},{2,18},{10... | collective-permute-start | bytes 3145736 | tf_op jit(solution)/shard_map/ppermute | solution.py:28
  3.1 91.3 %collective-permute-start.2 = (bf16[256,2048]{1,0:T(8,128)(2,1)}, bf16[256,2048]{1,0:T(8,128)(2,1)}, u32[]{:S(2)}, u32[]{:S(2)}) collective-permute-start(bf16[256,2048]{1,0:T(8,128)(2,1)} %bitcast.221), channel_id=1, source_target_pairs={{0,24},{8,0},{16,8},{24,16},{1,25},{9,1},{17,9},{25,17},{2,26},{10... | collective-permute-start | bytes 3145736 | tf_op jit(solution)/shard_map/ppermute | solution.py:28
  16.8 90.7 %collective-permute-start.3 = (bf16[256,2816]{0,1:T(8,128)(2,1)}, bf16[256,2816]{0,1:T(8,128)(2,1)}, u32[]{:S(2)}, u32[]{:S(2)}) collective-permute-start(bf16[256,2816]{0,1:T(8,128)(2,1)} %get-tuple-element.99), channel_id=1, source_target_pairs={{0,6},{1,7},{2,4},{3,5},{4,2},{5,3},{6,0},{7,1},{8,14},{9,15},{10,... | collective-permute-start | bytes 4325384 | tf_op jit(solution)/shard_map/ppermute | solution.py:23
  18.0 83.9 %collective-permute-start.19 = (bf16[256,2816]{0,1:T(8,128)(2,1)}, bf16[256,2816]{0,1:T(8,128)(2,1)}, u32[]{:S(2)}, u32[]{:S(2)}) collective-permute-start(bf16[256,2816]{0,1:T(8,128)(2,1)} %get-tuple-element.99), channel_id=1, source_target_pairs={{0,1},{1,0},{2,3},{3,2},{4,5},{5,4},{6,7},{7,6},{8,9},{9,8},{10,11... | collective-permute-start | bytes 4325384 | tf_op jit(solution)/shard_map/ppermute | solution.py:23
  94.4 33.0 %collective-permute-start.20 = (bf16[256,2816]{0,1:T(8,128)(2,1)}, bf16[256,2816]{0,1:T(8,128)(2,1)}, u32[]{:S(2)}, u32[]{:S(2)}) collective-permute-start(bf16[256,2816]{0,1:T(8,128)(2,1)} %get-tuple-element.99), channel_id=1, source_target_pairs={{0,2},{1,3},{2,0},{3,1},{4,6},{5,7},{6,4},{7,5},{8,10},{9,11},{10,... | collective-permute-start | bytes 4325384 | tf_op jit(solution)/shard_map/ppermute | solution.py:23
  94.7 35.7 %collective-permute-start.22 = (bf16[256,2816]{0,1:T(8,128)(2,1)}, bf16[256,2816]{0,1:T(8,128)(2,1)}, u32[]{:S(2)}, u32[]{:S(2)}) collective-permute-start(bf16[256,2816]{0,1:T(8,128)(2,1)} %get-tuple-element.99), channel_id=1, source_target_pairs={{0,4},{1,5},{2,6},{3,7},{4,0},{5,1},{6,2},{7,3},{8,12},{9,13},{10,... | collective-permute-start | bytes 4325384 | tf_op jit(solution)/shard_map/ppermute | solution.py:23
  97.3 34.7 %collective-permute-start.37 = (bf16[256,2048]{1,0:T(8,128)(2,1)}, bf16[256,2048]{1,0:T(8,128)(2,1)}, u32[]{:S(2)}, u32[]{:S(2)}) collective-permute-start(bf16[256,2048]{1,0:T(8,128)(2,1)} %bitcast.59), channel_id=1, source_target_pairs={{0,8},{8,16},{16,24},{24,0},{1,9},{9,17},{17,25},{25,1},{2,10},{10... | collective-permute-start | bytes 3145736 | tf_op jit(solution)/shard_map/ppermute | solution.py:28
  102.0 84.8 %collective-permute-start.38 = (bf16[256,2048]{1,0:T(8,128)(2,1)}, bf16[256,2048]{1,0:T(8,128)(2,1)}, u32[]{:S(2)}, u32[]{:S(2)}) collective-permute-start(bf16[256,2048]{1,0:T(8,128)(2,1)} %bitcast.59), channel_id=1, source_target_pairs={{0,16},{8,24},{16,0},{24,8},{1,17},{9,25},{17,1},{25,9},{2,18},{10... | collective-permute-start | bytes 3145736 | tf_op jit(solution)/shard_map/ppermute | solution.py:28
  107.5 90.3 %collective-permute-start.39 = (bf16[256,2048]{1,0:T(8,128)(2,1)}, bf16[256,2048]{1,0:T(8,128)(2,1)}, u32[]{:S(2)}, u32[]{:S(2)}) collective-permute-start(bf16[256,2048]{1,0:T(8,128)(2,1)} %bitcast.59), channel_id=1, source_target_pairs={{0,24},{8,0},{16,8},{24,16},{1,25},{9,1},{17,9},{25,17},{2,26},{10... | collective-permute-start | bytes 3145736 | tf_op jit(solution)/shard_map/ppermute | solution.py:28
  127.4 72.3 %collective-permute-start.4 = (bf16[256,1536]{0,1:T(8,128)(2,1)}, bf16[256,1536]{0,1:T(8,128)(2,1)}, u32[]{:S(2)}, u32[]{:S(2)}) collective-permute-start(bf16[256,1536]{0,1:T(8,128)(2,1)} %bitcast.8), channel_id=1, source_target_pairs={{0,1},{1,0},{2,3},{3,2},{4,5},{5,4},{6,7},{7,6},{8,9},{9,8},{10,11... | collective-permute-start | bytes 2359304 | tf_op jit(solution)/shard_map/ppermute | solution.py:23
  130.4 69.4 %collective-permute-start.5 = (bf16[256,1536]{0,1:T(8,128)(2,1)}, bf16[256,1536]{0,1:T(8,128)(2,1)}, u32[]{:S(2)}, u32[]{:S(2)}) collective-permute-start(bf16[256,1536]{0,1:T(8,128)(2,1)} %bitcast.8), channel_id=1, source_target_pairs={{0,2},{1,3},{2,0},{3,1},{4,6},{5,7},{6,4},{7,5},{8,10},{9,11},{10,... | collective-permute-start | bytes 2359304 | tf_op jit(solution)/shard_map/ppermute | solution.py:23
  132.0 78.7 %collective-permute-start.7 = (bf16[256,1536]{0,1:T(8,128)(2,1)}, bf16[256,1536]{0,1:T(8,128)(2,1)}, u32[]{:S(2)}, u32[]{:S(2)}) collective-permute-start(bf16[256,1536]{0,1:T(8,128)(2,1)} %bitcast.8), channel_id=1, source_target_pairs={{0,4},{1,5},{2,6},{3,7},{4,0},{5,1},{6,2},{7,3},{8,12},{9,13},{10,... | collective-permute-start | bytes 2359304 | tf_op jit(solution)/shard_map/ppermute | solution.py:23
  186.8 22.6 %collective-permute-start.9 = (bf16[256,1536]{0,1:T(8,128)(2,1)}, bf16[256,1536]{0,1:T(8,128)(2,1)}, u32[]{:S(2)}, u32[]{:S(2)}) collective-permute-start(bf16[256,1536]{0,1:T(8,128)(2,1)} %bitcast.8), channel_id=1, source_target_pairs={{0,6},{1,7},{2,4},{3,5},{4,2},{5,3},{6,0},{7,1},{8,14},{9,15},{10,... | collective-permute-start | bytes 2359304 | tf_op jit(solution)/shard_map/ppermute | solution.py:23
  197.9 27.2 %collective-permute-start.21 = (bf16[256,2816]{0,1:T(8,128)(2,1)}, bf16[256,2816]{0,1:T(8,128)(2,1)}, u32[]{:S(2)}, u32[]{:S(2)}) collective-permute-start(bf16[256,2816]{0,1:T(8,128)(2,1)} %collective-permute-done.20), channel_id=1, source_target_pairs={{0,1},{1,0},{2,3},{3,2},{4,5},{5,4},{6,7},{7,6},{8,9},{9,8},{10,11... | collective-permute-start | bytes 4325384 | tf_op jit(solution)/shard_map/ppermute | solution.py:23
  199.7 29.0 %collective-permute-start.23 = (bf16[256,2816]{0,1:T(8,128)(2,1)}, bf16[256,2816]{0,1:T(8,128)(2,1)}, u32[]{:S(2)}, u32[]{:S(2)}) collective-permute-start(bf16[256,2816]{0,1:T(8,128)(2,1)} %collective-permute-done.22), channel_id=1, source_target_pairs={{0,1},{1,0},{2,3},{3,2},{4,5},{5,4},{6,7},{7,6},{8,9},{9,8},{10,11... | collective-permute-start | bytes 4325384 | tf_op jit(solution)/shard_map/ppermute | solution.py:23
  199.8 31.7 %collective-permute-start.24 = (bf16[256,2816]{0,1:T(8,128)(2,1)}, bf16[256,2816]{0,1:T(8,128)(2,1)}, u32[]{:S(2)}, u32[]{:S(2)}) collective-permute-start(bf16[256,2816]{0,1:T(8,128)(2,1)} %collective-permute-done.3), channel_id=1, source_target_pairs={{0,1},{1,0},{2,3},{3,2},{4,5},{5,4},{6,7},{7,6},{8,9},{9,8},{10,11... | collective-permute-start | bytes 4325384 | tf_op jit(solution)/shard_map/ppermute | solution.py:23
  209.4 44.2 %collective-permute-start.11 = (bf16[176,2048]{1,0:T(8,128)(2,1)}, bf16[176,2048]{1,0:T(8,128)(2,1)}, u32[]{:S(2)}, u32[]{:S(2)}) collective-permute-start(bf16[176,2048]{1,0:T(8,128)(2,1)} %constant_dynamic-slice_fusion.11), channel_id=1, source_target_pairs={{0,6},{1,7},{2,4},{3,5},{4,2},{5,3},{6,0},{7,1},{8,14},{9,15},{10,... | collective-permute-start | bytes 2162696 | tf_op jit(solution)/shard_map/ppermute | solution.py:23
  210.7 42.9 %collective-permute-start.25 = (bf16[176,2048]{1,0:T(8,128)(2,1)}, bf16[176,2048]{1,0:T(8,128)(2,1)}, u32[]{:S(2)}, u32[]{:S(2)}) collective-permute-start(bf16[176,2048]{1,0:T(8,128)(2,1)} %constant_dynamic-slice_fusion.11), channel_id=1, source_target_pairs={{0,1},{1,0},{2,3},{3,2},{4,5},{5,4},{6,7},{7,6},{8,9},{9,8},{10,11... | collective-permute-start | bytes 2162696 | tf_op jit(solution)/shard_map/ppermute | solution.py:23
  225.1 32.3 %collective-permute-start.26 = (bf16[176,2048]{1,0:T(8,128)(2,1)}, bf16[176,2048]{1,0:T(8,128)(2,1)}, u32[]{:S(2)}, u32[]{:S(2)}) collective-permute-start(bf16[176,2048]{1,0:T(8,128)(2,1)} %constant_dynamic-slice_fusion.11), channel_id=1, source_target_pairs={{0,2},{1,3},{2,0},{3,1},{4,6},{5,7},{6,4},{7,5},{8,10},{9,11},{10,... | collective-permute-start | bytes 2162696 | tf_op jit(solution)/shard_map/ppermute | solution.py:23
  228.8 86.9 %collective-permute-start.28 = (bf16[176,2048]{1,0:T(8,128)(2,1)}, bf16[176,2048]{1,0:T(8,128)(2,1)}, u32[]{:S(2)}, u32[]{:S(2)}) collective-permute-start(bf16[176,2048]{1,0:T(8,128)(2,1)} %constant_dynamic-slice_fusion.11), channel_id=1, source_target_pairs={{0,4},{1,5},{2,6},{3,7},{4,0},{5,1},{6,2},{7,3},{8,12},{9,13},{10,... | collective-permute-start | bytes 2162696 | tf_op jit(solution)/shard_map/ppermute | solution.py:23
  231.5 28.6 %collective-permute-start.6 = (bf16[256,1536]{0,1:T(8,128)(2,1)}, bf16[256,1536]{0,1:T(8,128)(2,1)}, u32[]{:S(2)}, u32[]{:S(2)}) collective-permute-start(bf16[256,1536]{0,1:T(8,128)(2,1)} %collective-permute-done.5), channel_id=1, source_target_pairs={{0,1},{1,0},{2,3},{3,2},{4,5},{5,4},{6,7},{7,6},{8,9},{9,8},{10,11... | collective-permute-start | bytes 2359304 | tf_op jit(solution)/shard_map/ppermute | solution.py:23
  257.4 55.3 %collective-permute-start.12 = (bf16[64,2048]{1,0:T(8,128)(2,1)}, bf16[64,2048]{1,0:T(8,128)(2,1)}, u32[]{:S(2)}, u32[]{:S(2)}) collective-permute-start(bf16[64,2048]{1,0:T(8,128)(2,1)} %constant_dynamic-slice_fusion.12), channel_id=1, source_target_pairs={{0,1},{1,0},{2,3},{3,2},{4,5},{5,4},{6,7},{7,6},{8,9},{9,8},{10,11... | collective-permute-start | bytes 786440 | tf_op jit(solution)/shard_map/ppermute | solution.py:23
  260.1 53.5 %collective-permute-start.13 = (bf16[64,2048]{1,0:T(8,128)(2,1)}, bf16[64,2048]{1,0:T(8,128)(2,1)}, u32[]{:S(2)}, u32[]{:S(2)}) collective-permute-start(bf16[64,2048]{1,0:T(8,128)(2,1)} %constant_dynamic-slice_fusion.12), channel_id=1, source_target_pairs={{0,2},{1,3},{2,0},{3,1},{4,6},{5,7},{6,4},{7,5},{8,10},{9,11},{10,... | collective-permute-start | bytes 786440 | tf_op jit(solution)/shard_map/ppermute | solution.py:23
  262.8 53.4 %collective-permute-start.15 = (bf16[64,2048]{1,0:T(8,128)(2,1)}, bf16[64,2048]{1,0:T(8,128)(2,1)}, u32[]{:S(2)}, u32[]{:S(2)}) collective-permute-start(bf16[64,2048]{1,0:T(8,128)(2,1)} %constant_dynamic-slice_fusion.12), channel_id=1, source_target_pairs={{0,4},{1,5},{2,6},{3,7},{4,0},{5,1},{6,2},{7,3},{8,12},{9,13},{10,... | collective-permute-start | bytes 786440 | tf_op jit(solution)/shard_map/ppermute | solution.py:23
  266.3 51.4 %collective-permute-start.17 = (bf16[64,2048]{1,0:T(8,128)(2,1)}, bf16[64,2048]{1,0:T(8,128)(2,1)}, u32[]{:S(2)}, u32[]{:S(2)}) collective-permute-start(bf16[64,2048]{1,0:T(8,128)(2,1)} %constant_dynamic-slice_fusion.12), channel_id=1, source_target_pairs={{0,6},{1,7},{2,4},{3,5},{4,2},{5,3},{6,0},{7,1},{8,14},{9,15},{10,... | collective-permute-start | bytes 786440 | tf_op jit(solution)/shard_map/ppermute | solution.py:23
  312.7 73.7 %collective-permute-start.27 = (bf16[176,2048]{1,0:T(8,128)(2,1)}, bf16[176,2048]{1,0:T(8,128)(2,1)}, u32[]{:S(2)}, u32[]{:S(2)}) collective-permute-start(bf16[176,2048]{1,0:T(8,128)(2,1)} %collective-permute-done.26), channel_id=1, source_target_pairs={{0,1},{1,0},{2,3},{3,2},{4,5},{5,4},{6,7},{7,6},{8,9},{9,8},{10,11... | collective-permute-start | bytes 2162696 | tf_op jit(solution)/shard_map/ppermute | solution.py:23
  315.7 79.0 %collective-permute-start.30 = (bf16[176,2048]{1,0:T(8,128)(2,1)}, bf16[176,2048]{1,0:T(8,128)(2,1)}, u32[]{:S(2)}, u32[]{:S(2)}) collective-permute-start(bf16[176,2048]{1,0:T(8,128)(2,1)} %collective-permute-done.11), channel_id=1, source_target_pairs={{0,1},{1,0},{2,3},{3,2},{4,5},{5,4},{6,7},{7,6},{8,9},{9,8},{10,11... | collective-permute-start | bytes 2162696 | tf_op jit(solution)/shard_map/ppermute | solution.py:23
  316.2 74.4 %collective-permute-start.29 = (bf16[176,2048]{1,0:T(8,128)(2,1)}, bf16[176,2048]{1,0:T(8,128)(2,1)}, u32[]{:S(2)}, u32[]{:S(2)}) collective-permute-start(bf16[176,2048]{1,0:T(8,128)(2,1)} %collective-permute-done.28), channel_id=1, source_target_pairs={{0,1},{1,0},{2,3},{3,2},{4,5},{5,4},{6,7},{7,6},{8,9},{9,8},{10,11... | collective-permute-start | bytes 2162696 | tf_op jit(solution)/shard_map/ppermute | solution.py:23
  317.7 186.0 %collective-permute-start.53 = (bf16[4,64,2048]{2,1,0:T(8,128)(2,1)}, bf16[4,64,2048]{2,1,0:T(8,128)(2,1)}, u32[]{:S(2)}, u32[]{:S(2)}) collective-permute-start(bf16[4,64,2048]{2,1,0:T(8,128)(2,1)} %dynamic-slice_bitcast_fusion.4), channel_id=1, source_target_pairs={{0,1},{1,0},{2,3},{3,2},{4,5},{5,4},{6,7},{7,6},{8,9},{9,8},{10,11... | collective-permute-start | bytes 3145736 | tf_op jit(solution)/shard_map/ppermute | solution.py:23
  383.2 281.4 %collective-permute-start.46 = (bf16[4,256,1536]{1,2,0:T(8,128)(2,1)}, bf16[4,256,1536]{1,2,0:T(8,128)(2,1)}, u32[]{:S(2)}, u32[]{:S(2)}) collective-permute-start(bf16[4,256,1536]{1,2,0:T(8,128)(2,1)} %bitcast.245), channel_id=1, source_target_pairs={{0,1},{1,0},{2,3},{3,2},{4,5},{5,4},{6,7},{7,6},{8,9},{9,8},{10,11... | collective-permute-start | bytes 9437192 | tf_op jit(solution)/shard_map/ppermute | solution.py:23
  482.3 114.7 %collective-permute-start.40 = (bf16[256,2048]{1,0:T(8,128)(2,1)}, bf16[256,2048]{1,0:T(8,128)(2,1)}, u32[]{:S(2)}, u32[]{:S(2)}) collective-permute-start(bf16[256,2048]{1,0:T(8,128)(2,1)} %get-tuple-element.82), channel_id=1, source_target_pairs={{24,16},{25,17},{26,18},{27,19},{28,20},{29,21},{30,22},{31,23}} | collective-permute-start | bytes 3145736 | tf_op jit(solution)/shard_map/ppermute | solution.py:93
  515.0 95.5 %collective-permute-start.43 = (bf16[256,2048]{1,0:T(8,128)(2,1)S(1)}, bf16[256,2048]{1,0:T(8,128)(2,1)}, u32[]{:S(2)}, u32[]{:S(2)}) collective-permute-start(bf16[256,2048]{1,0:T(8,128)(2,1)S(1)} %get-tuple-element.83), channel_id=1, source_target_pairs={{0,8},{1,9},{2,10},{3,11},{4,12},{5,13},{6,14},{7,15}} | collective-permute-start | bytes 3145736 | tf_op jit(solution)/shard_map/ppermute | solution.py:94
  521.0 85.8 %collective-permute-start.31 = (bf16[256,2048]{1,0:T(8,128)(2,1)}, bf16[256,2048]{1,0:T(8,128)(2,1)}, u32[]{:S(2)}, u32[]{:S(2)}) collective-permute-start(bf16[256,2048]{1,0:T(8,128)(2,1)} %get-tuple-element.86), channel_id=1, source_target_pairs={{24,16},{25,17},{26,18},{27,19},{28,20},{29,21},{30,22},{31,23}} | collective-permute-start | bytes 3145736 | tf_op jit(solution)/shard_map/ppermute | solution.py:93
  523.7 58.9 %collective-permute-start.57 = (bf16[64,2048]{1,0:T(8,128)(2,1)}, bf16[64,2048]{1,0:T(8,128)(2,1)S(1)}, u32[]{:S(2)}, u32[]{:S(2)}) collective-permute-start(bf16[64,2048]{1,0:T(8,128)(2,1)} %get-tuple-element.69), channel_id=1, source_target_pairs={{0,8},{8,16},{16,24},{24,0},{1,9},{9,17},{17,25},{25,1},{2,10},{10... | collective-permute-start | bytes 786440 | tf_op jit(solution)/shard_map/ppermute | solution.py:28
  596.5 64.1 %collective-permute-start.67 = (bf16[4,176,2048]{2,1,0:T(8,128)(2,1)}, bf16[4,176,2048]{2,1,0:T(8,128)(2,1)S(1)}, u32[]{:S(2)}, u32[]{:S(2)}) collective-permute-start(bf16[4,176,2048]{2,1,0:T(8,128)(2,1)} %dynamic-slice_bitcast_fusion), channel_id=1, source_target_pairs={{0,1},{1,0},{2,3},{3,2},{4,5},{5,4},{6,7},{7,6},{8,9},{9,8},{10,11... | collective-permute-start | bytes 8650760 | tf_op jit(solution)/shard_map/ppermute | solution.py:23
  605.5 26.4 %collective-permute-start.41 = (bf16[256,2048]{1,0:T(8,128)(2,1)S(1)}, bf16[256,2048]{1,0:T(8,128)(2,1)S(1)}, u32[]{:S(2)}, u32[]{:S(2)}) collective-permute-start(bf16[256,2048]{1,0:T(8,128)(2,1)S(1)} %add_convert_fusion.3), channel_id=1, source_target_pairs={{16,8},{24,16},{17,9},{25,17},{18,10},{26,18},{19,11},{27,19},{20,... | collective-permute-start | bytes 3145736 | tf_op jit(solution)/shard_map/ppermute | solution.py:93
  606.8 30.7 %collective-permute-start.34 = (bf16[256,2048]{1,0:T(8,128)(2,1)S(1)}, bf16[256,2048]{1,0:T(8,128)(2,1)S(1)}, u32[]{:S(2)}, u32[]{:S(2)}) collective-permute-start(bf16[256,2048]{1,0:T(8,128)(2,1)S(1)} %copy-done.31), channel_id=1, source_target_pairs={{0,8},{1,9},{2,10},{3,11},{4,12},{5,13},{6,14},{7,15}} | collective-permute-start | bytes 3145736 | tf_op jit(solution)/shard_map/ppermute | solution.py:94
  610.5 43.8 %collective-permute-start.32 = (bf16[256,2048]{1,0:T(8,128)(2,1)S(1)}, bf16[256,2048]{1,0:T(8,128)(2,1)S(1)}, u32[]{:S(2)}, u32[]{:S(2)}) collective-permute-start(bf16[256,2048]{1,0:T(8,128)(2,1)S(1)} %add_convert_fusion.7), channel_id=1, source_target_pairs={{16,8},{24,16},{17,9},{25,17},{18,10},{26,18},{19,11},{27,19},{20,... | collective-permute-start | bytes 3145736 | tf_op jit(solution)/shard_map/ppermute | solution.py:93
  631.9 191.3 %collective-permute-start.60 = (bf16[4,256,2816]{1,2,0:T(8,128)(2,1)}, bf16[4,256,2816]{1,2,0:T(8,128)(2,1)}, u32[]{:S(2)}, u32[]{:S(2)}) collective-permute-start(bf16[4,256,2816]{1,2,0:T(8,128)(2,1)} %bitcast.93), channel_id=1, source_target_pairs={{0,1},{1,0},{2,3},{3,2},{4,5},{5,4},{6,7},{7,6},{8,9},{9,8},{10,11... | collective-permute-start | bytes 17301512 | tf_op jit(solution)/shard_map/ppermute | solution.py:23
  637.6 30.0 %collective-permute-start.44 = (bf16[256,2048]{1,0:T(8,128)(2,1)S(1)}, bf16[256,2048]{1,0:T(8,128)(2,1)S(1)}, u32[]{:S(2)}, u32[]{:S(2)}) collective-permute-start(bf16[256,2048]{1,0:T(8,128)(2,1)S(1)} %get-tuple-element.81), channel_id=1, source_target_pairs={{8,16},{0,8},{9,17},{1,9},{10,18},{2,10},{11,19},{3,11},{12,20},{4... | collective-permute-start | bytes 3145736 | tf_op jit(solution)/shard_map/ppermute | solution.py:94
  656.1 31.0 %collective-permute-start.35 = (bf16[256,2048]{1,0:T(8,128)(2,1)}, bf16[256,2048]{1,0:T(8,128)(2,1)S(1)}, u32[]{:S(2)}, u32[]{:S(2)}) collective-permute-start(bf16[256,2048]{1,0:T(8,128)(2,1)} %get-tuple-element.85), channel_id=1, source_target_pairs={{8,16},{0,8},{9,17},{1,9},{10,18},{2,10},{11,19},{3,11},{12,20},{4... | collective-permute-start | bytes 3145736 | tf_op jit(solution)/shard_map/ppermute | solution.py:94
  663.4 25.1 %collective-permute-start.70 = (bf16[176,2048]{1,0:T(8,128)(2,1)}, bf16[176,2048]{1,0:T(8,128)(2,1)}, u32[]{:S(2)}, u32[]{:S(2)}) collective-permute-start(bf16[176,2048]{1,0:T(8,128)(2,1)} %get-tuple-element.97), channel_id=1, source_target_pairs={{0,6},{1,7},{2,4},{3,5},{4,2},{5,3},{6,0},{7,1},{8,14},{9,15},{10,... | collective-permute-start | bytes 2162696 | tf_op jit(solution)/shard_map/ppermute | solution.py:23
  664.6 35.5 %collective-permute-start.69 = (bf16[176,2048]{1,0:T(8,128)(2,1)}, bf16[176,2048]{1,0:T(8,128)(2,1)}, u32[]{:S(2)}, u32[]{:S(2)}) collective-permute-start(bf16[176,2048]{1,0:T(8,128)(2,1)} %get-tuple-element.98), channel_id=1, source_target_pairs={{0,4},{1,5},{2,6},{3,7},{4,0},{5,1},{6,2},{7,3},{8,12},{9,13},{10,... | collective-permute-start | bytes 2162696 | tf_op jit(solution)/shard_map/ppermute | solution.py:23
  668.5 31.9 %collective-permute-start.68 = (bf16[176,2048]{1,0:T(8,128)(2,1)S(1)}, bf16[176,2048]{1,0:T(8,128)(2,1)S(1)}, u32[]{:S(2)}, u32[]{:S(2)}) collective-permute-start(bf16[176,2048]{1,0:T(8,128)(2,1)S(1)} %copy-done.32), channel_id=1, source_target_pairs={{0,2},{1,3},{2,0},{3,1},{4,6},{5,7},{6,4},{7,5},{8,10},{9,11},{10,... | collective-permute-start | bytes 2162696 | tf_op jit(solution)/shard_map/ppermute | solution.py:23
  687.0 25.9 %collective-permute-start.49 = (bf16[256,1536]{0,1:T(8,128)(2,1)S(1)}, bf16[256,1536]{0,1:T(8,128)(2,1)S(1)}, u32[]{:S(2)}, u32[]{:S(2)}) collective-permute-start(bf16[256,1536]{0,1:T(8,128)(2,1)S(1)} %get-tuple-element.94), channel_id=1, source_target_pairs={{0,6},{1,7},{2,4},{3,5},{4,2},{5,3},{6,0},{7,1},{8,14},{9,15},{10,... | collective-permute-start | bytes 2359304 | tf_op jit(solution)/shard_map/ppermute | solution.py:23
  688.5 43.2 %collective-permute-start.48 = (bf16[256,1536]{0,1:T(8,128)(2,1)S(1)}, bf16[256,1536]{0,1:T(8,128)(2,1)S(1)}, u32[]{:S(2)}, u32[]{:S(2)}) collective-permute-start(bf16[256,1536]{0,1:T(8,128)(2,1)S(1)} %get-tuple-element.95), channel_id=1, source_target_pairs={{0,4},{1,5},{2,6},{3,7},{4,0},{5,1},{6,2},{7,3},{8,12},{9,13},{10,... | collective-permute-start | bytes 2359304 | tf_op jit(solution)/shard_map/ppermute | solution.py:23
  700.1 33.5 %collective-permute-start.47 = (bf16[256,1536]{0,1:T(8,128)(2,1)S(1)}, bf16[256,1536]{0,1:T(8,128)(2,1)S(1)}, u32[]{:S(2)}, u32[]{:S(2)}) collective-permute-start(bf16[256,1536]{0,1:T(8,128)(2,1)S(1)} %get-tuple-element.93), channel_id=1, source_target_pairs={{0,2},{1,3},{2,0},{3,1},{4,6},{5,7},{6,4},{7,5},{8,10},{9,11},{10,... | collective-permute-start | bytes 2359304 | tf_op jit(solution)/shard_map/ppermute | solution.py:23
  700.5 38.2 %collective-permute-start.42 = (bf16[256,2048]{1,0:T(8,128)(2,1)S(1)}, bf16[256,2048]{1,0:T(8,128)(2,1)S(1)}, u32[]{:S(2)}, u32[]{:S(2)}) collective-permute-start(bf16[256,2048]{1,0:T(8,128)(2,1)S(1)} %get-tuple-element.80), channel_id=1, source_target_pairs={{8,0},{16,8},{24,16},{9,1},{17,9},{25,17},{10,2},{18,10},{26,18},{... | collective-permute-start | bytes 3145736 | tf_op jit(solution)/shard_map/ppermute | solution.py:93
  712.9 25.7 %collective-permute-start.45 = (bf16[256,2048]{1,0:T(8,128)(2,1)S(1)}, bf16[256,2048]{1,0:T(8,128)(2,1)S(1)}, u32[]{:S(2)}, u32[]{:S(2)}) collective-permute-start(bf16[256,2048]{1,0:T(8,128)(2,1)S(1)} %add_convert_fusion), channel_id=1, source_target_pairs={{16,24},{8,16},{0,8},{17,25},{9,17},{1,9},{18,26},{10,18},{2,10},{... | collective-permute-start | bytes 3145736 | tf_op jit(solution)/shard_map/ppermute | solution.py:94
  731.7 27.0 %collective-permute-start.33 = (bf16[256,2048]{1,0:T(8,128)(2,1)S(1)}, bf16[256,2048]{1,0:T(8,128)(2,1)S(1)}, u32[]{:S(2)}, u32[]{:S(2)}) collective-permute-start(bf16[256,2048]{1,0:T(8,128)(2,1)S(1)} %get-tuple-element.84), channel_id=1, source_target_pairs={{8,0},{16,8},{24,16},{9,1},{17,9},{25,17},{10,2},{18,10},{26,18},{... | collective-permute-start | bytes 3145736 | tf_op jit(solution)/shard_map/ppermute | solution.py:93
  733.7 27.1 %collective-permute-start.36 = (bf16[256,2048]{1,0:T(8,128)(2,1)S(1)}, bf16[256,2048]{1,0:T(8,128)(2,1)S(1)}, u32[]{:S(2)}, u32[]{:S(2)}) collective-permute-start(bf16[256,2048]{1,0:T(8,128)(2,1)S(1)} %add_convert_fusion.4), channel_id=1, source_target_pairs={{16,24},{8,16},{0,8},{17,25},{9,17},{1,9},{18,26},{10,18},{2,10},{... | collective-permute-start | bytes 3145736 | tf_op jit(solution)/shard_map/ppermute | solution.py:94
  738.7 37.7 %collective-permute-start.71 = (bf16[176,2048]{1,0:T(8,128)(2,1)S(1)}, bf16[176,2048]{1,0:T(8,128)(2,1)S(1)}, u32[]{:S(2)}, u32[]{:S(2)}) collective-permute-start(bf16[176,2048]{1,0:T(8,128)(2,1)S(1)} %get-tuple-element.65), channel_id=1, source_target_pairs={{0,8},{8,16},{16,24},{24,0},{1,9},{9,17},{17,25},{25,1},{2,10},{10... | collective-permute-start | bytes 2162696 | tf_op jit(solution)/shard_map/ppermute | solution.py:28
  738.7 82.5 %collective-permute-start.72 = (bf16[176,2048]{1,0:T(8,128)(2,1)S(1)}, bf16[176,2048]{1,0:T(8,128)(2,1)}, u32[]{:S(2)}, u32[]{:S(2)}) collective-permute-start(bf16[176,2048]{1,0:T(8,128)(2,1)S(1)} %get-tuple-element.65), channel_id=1, source_target_pairs={{0,16},{8,24},{16,0},{24,8},{1,17},{9,25},{17,1},{25,9},{2,18},{10... | collective-permute-start | bytes 2162696 | tf_op jit(solution)/shard_map/ppermute | solution.py:28
  758.8 94.8 %collective-permute-start.73 = (bf16[176,2048]{1,0:T(8,128)(2,1)S(1)}, bf16[176,2048]{1,0:T(8,128)(2,1)}, u32[]{:S(2)}, u32[]{:S(2)}) collective-permute-start(bf16[176,2048]{1,0:T(8,128)(2,1)S(1)} %get-tuple-element.65), channel_id=1, source_target_pairs={{0,24},{8,0},{16,8},{24,16},{1,25},{9,1},{17,9},{25,17},{2,26},{10... | collective-permute-start | bytes 2162696 | tf_op jit(solution)/shard_map/ppermute | solution.py:28
  760.8 102.6 %collective-permute-start.50 = (bf16[256,1536]{0,1:T(8,128)(2,1)}, bf16[256,1536]{0,1:T(8,128)(2,1)}, u32[]{:S(2)}, u32[]{:S(2)}) collective-permute-start(bf16[256,1536]{0,1:T(8,128)(2,1)} %get-tuple-element.71), channel_id=1, source_target_pairs={{0,8},{8,16},{16,24},{24,0},{1,9},{9,17},{17,25},{25,1},{2,10},{10... | collective-permute-start | bytes 2359304 | tf_op jit(solution)/shard_map/ppermute | solution.py:28
  776.4 125.3 %collective-permute-start.51 = (bf16[256,1536]{0,1:T(8,128)(2,1)}, bf16[256,1536]{0,1:T(8,128)(2,1)}, u32[]{:S(2)}, u32[]{:S(2)}) collective-permute-start(bf16[256,1536]{0,1:T(8,128)(2,1)} %get-tuple-element.71), channel_id=1, source_target_pairs={{0,16},{8,24},{16,0},{24,8},{1,17},{9,25},{17,1},{25,9},{2,18},{10... | collective-permute-start | bytes 2359304 | tf_op jit(solution)/shard_map/ppermute | solution.py:28
  832.5 32.3 %collective-permute-start.63 = (bf16[256,2816]{0,1:T(8,128)(2,1)S(1)}, bf16[256,2816]{0,1:T(8,128)(2,1)S(1)}, u32[]{:S(2)}, u32[]{:S(2)}) collective-permute-start(bf16[256,2816]{0,1:T(8,128)(2,1)S(1)} %get-tuple-element.91), channel_id=1, source_target_pairs={{0,6},{1,7},{2,4},{3,5},{4,2},{5,3},{6,0},{7,1},{8,14},{9,15},{10,... | collective-permute-start | bytes 4325384 | tf_op jit(solution)/shard_map/ppermute | solution.py:23
  833.7 64.1 %collective-permute-start.62 = (bf16[256,2816]{0,1:T(8,128)(2,1)S(1)}, bf16[256,2816]{0,1:T(8,128)(2,1)S(1)}, u32[]{:S(2)}, u32[]{:S(2)}) collective-permute-start(bf16[256,2816]{0,1:T(8,128)(2,1)S(1)} %get-tuple-element.92), channel_id=1, source_target_pairs={{0,4},{1,5},{2,6},{3,7},{4,0},{5,1},{6,2},{7,3},{8,12},{9,13},{10,... | collective-permute-start | bytes 4325384 | tf_op jit(solution)/shard_map/ppermute | solution.py:23
  853.6 44.3 %collective-permute-start.61 = (bf16[256,2816]{0,1:T(8,128)(2,1)S(1)}, bf16[256,2816]{0,1:T(8,128)(2,1)S(1)}, u32[]{:S(2)}, u32[]{:S(2)}) collective-permute-start(bf16[256,2816]{0,1:T(8,128)(2,1)S(1)} %get-tuple-element.90), channel_id=1, source_target_pairs={{0,2},{1,3},{2,0},{3,1},{4,6},{5,7},{6,4},{7,5},{8,10},{9,11},{10,... | collective-permute-start | bytes 4325384 | tf_op jit(solution)/shard_map/ppermute | solution.py:23
  863.4 43.3 %collective-permute-start.52 = (bf16[256,1536]{0,1:T(8,128)(2,1)}, bf16[256,1536]{0,1:T(8,128)(2,1)S(1)}, u32[]{:S(2)}, u32[]{:S(2)}) collective-permute-start(bf16[256,1536]{0,1:T(8,128)(2,1)} %get-tuple-element.71), channel_id=1, source_target_pairs={{0,24},{8,0},{16,8},{24,16},{1,25},{9,1},{17,9},{25,17},{2,26},{10... | collective-permute-start | bytes 2359304 | tf_op jit(solution)/shard_map/ppermute | solution.py:28
  901.6 33.0 %collective-permute-start.64 = (bf16[256,2816]{0,1:T(8,128)(2,1)}, bf16[256,2816]{0,1:T(8,128)(2,1)}, u32[]{:S(2)}, u32[]{:S(2)}) collective-permute-start(bf16[256,2816]{0,1:T(8,128)(2,1)} %get-tuple-element.67), channel_id=1, source_target_pairs={{0,8},{8,16},{16,24},{24,0},{1,9},{9,17},{17,25},{25,1},{2,10},{10... | collective-permute-start | bytes 4325384 | tf_op jit(solution)/shard_map/ppermute | solution.py:28
  903.4 119.0 %collective-permute-start.65 = (bf16[256,2816]{0,1:T(8,128)(2,1)}, bf16[256,2816]{0,1:T(8,128)(2,1)}, u32[]{:S(2)}, u32[]{:S(2)}) collective-permute-start(bf16[256,2816]{0,1:T(8,128)(2,1)} %get-tuple-element.67), channel_id=1, source_target_pairs={{0,16},{8,24},{16,0},{24,8},{1,17},{9,25},{17,1},{25,9},{2,18},{10... | collective-permute-start | bytes 4325384 | tf_op jit(solution)/shard_map/ppermute | solution.py:28
  917.6 112.2 %collective-permute-start.66 = (bf16[256,2816]{0,1:T(8,128)(2,1)}, bf16[256,2816]{0,1:T(8,128)(2,1)S(1)}, u32[]{:S(2)}, u32[]{:S(2)}) collective-permute-start(bf16[256,2816]{0,1:T(8,128)(2,1)} %get-tuple-element.67), channel_id=1, source_target_pairs={{0,24},{8,0},{16,8},{24,16},{1,25},{9,1},{17,9},{25,17},{2,26},{10... | collective-permute-start | bytes 4325384 | tf_op jit(solution)/shard_map/ppermute | solution.py:28
  (60 other events, 1275.1 us)

commit v2 on v1

--- a/solution.py
+++ b/solution.py
@@ -204,6 +204,320 @@
     )(q, k, v, d_attended, attended, lse, *tables)
 
 
+MESH = pl.DeviceIdType.MESH
+TILE = 256
+HALF = 128
+DEEP = 4
+LAG = 2
+
+
+def rows_of(shard, part):
+    return slice(shard * part, (shard + 1) * part)
+
+
+def gradients_kernel(
+    hid_t, att_t, cot, norm_t, d_gate, d_up, d_mixed, pieces,
+    partial, theirs, pair, landed, total,
+    core_send, core_recv, chip_send, chip_recv, line_send, line_recv, own_sem,
+):
+    count = pieces.shape[0]
+    chunks = pieces.shape[1]
+    shards = 2 * partial.shape[1]
+    chips = shards // 2
+    place, me = lax.axis_index("ctx"), lax.axis_index("fsdp")
+    chip, core = me // 2, me % 2
+    ff_part, attn_part = hid_t.shape[0] // shards, att_t.shape[0] // shards
+    cot_chunks = cot.shape[1] // TILE
+    inner_chunks = d_gate.shape[1] // HALF
+
+    def core_copy(i):
+        return pltpu.make_async_remote_copy(
+            src_ref=partial.at[i % 2, :, 1 - core],
+            dst_ref=theirs.at[i % DEEP],
+            send_sem=core_send.at[i % 2],
+            recv_sem=core_recv.at[i % DEEP],
+            device_id=(place, me + 1 - 2 * core),
+            device_id_type=MESH,
+        )
+
+    def chip_of(m):
+        low = (chip % 2 + m % 2) % 2
+        high = (chip // 2 + m // 2) % 2
+        return 2 * high + low
+
+    def chip_copy(j, m):
+        return pltpu.make_async_remote_copy(
+            src_ref=pair.at[j % 2, chip_of(m)],
+            dst_ref=landed.at[j % DEEP, m - 1],
+            send_sem=chip_send.at[j % 2, m - 1],
+            recv_sem=chip_recv.at[j % DEEP, m - 1],
+            device_id=(place, 2 * chip_of(m) + core),
+            device_id_type=MESH,
+        )
+
+    def line_copy(way, hop, k):
+        ahead = 1 - 2 * way
+        origin = place - (hop - 1) * ahead
+        return pltpu.make_async_remote_copy(
+            src_ref=total.at[k % DEEP] if hop == 1 else pieces.at[origin, k],
+            dst_ref=pieces.at[origin, k],
+            send_sem=line_send.at[way, hop - 1, k % DEEP],
+            recv_sem=line_recv.at[way, k, hop - 1],
+            device_id=(place + ahead, me),
+            device_id_type=MESH,
+        )
+
+    def sends(way, hop):
+        if way == 0:
+            return (place >= hop - 1) & (place <= count - 2)
+        return (place <= count - hop) & (place >= 1)
+
+    def lands(way, hop):
+        return place >= hop if way == 0 else place <= count - 1 - hop
+
+    def forward(hop, k):
+        for way in range(2):
+            if hop > 1:
+                @pl.when(lands(way, hop - 1))
+                def _():
+                    line_copy(way, hop - 1, k).wait_recv()
+
+            if hop < count:
+                @pl.when(sends(way, hop))
+                def _():
+                    @pl.when(k >= DEEP)
+                    def _():
+                        line_copy(way, hop, k - DEEP).wait_send()
+
+                    line_copy(way, hop, k).start()
+
+    def own_copy(k):
+        return pltpu.make_async_copy(total.at[k % DEEP], pieces.at[place, k], own_sem.at[k % DEEP])
+
+    partners = [(place, me + 1 - 2 * core)]
+    partners += [(place, 2 * chip_of(m) + core) for m in range(1, chips)]
+    partners += [((place + 1) % count, me), ((place + count - 1) % count, me)]
+    barrier = pltpu.get_barrier_semaphore()
+    for partner in partners:
+        pl.semaphore_signal(barrier, inc=1, device_id=partner, device_id_type=MESH)
+    pl.semaphore_wait(barrier, len(partners))
+    def store(i, shard, lo, value):
+        partial[i % 2, shard // 2, shard % 2, lo : lo + value.shape[0], :] = value
+
+    def from_norm(i, rhs):
+        for s in range(0, shards, 2):
+            rows = norm_t.shape[0] // shards
+            value = contract(norm_t[s * rows : (s + 2) * rows, :], rhs, ((1,), (0,))).astype(BF)
+            store(i, s, 0, value[:rows])
+            store(i, s + 1, 0, value[rows:])
+
+    def step(i, carry):
+        @pl.when(i < cot_chunks)
+        def _():
+            rhs = cot[:, pl.ds(pl.multiple_of(i * TILE, TILE), TILE)]
+            for s in range(0, shards, 4):
+                value = contract(hid_t[s * ff_part : (s + 4) * ff_part, :], rhs, ((1,), (0,))).astype(BF)
+                for t in range(4):
+                    store(i, s + t, 0, value[rows_of(t, ff_part)])
+            value = contract(att_t[...], rhs, ((1,), (0,))).astype(BF)
+            for s in range(shards):
+                store(i, s, ff_part, value[rows_of(s, attn_part)])
+
+        @pl.when((i >= cot_chunks) & (i < cot_chunks + inner_chunks))
+        def _():
+            at = pl.ds(pl.multiple_of((i - cot_chunks) * HALF, HALF), HALF)
+            from_norm(i, jnp.concatenate([d_gate[:, at], d_up[:, at]], axis=1))
+
+        @pl.when((i >= cot_chunks + inner_chunks) & (i < chunks))
+        def _():
+            at = pl.multiple_of((i - cot_chunks - inner_chunks) * TILE, TILE)
+            from_norm(i, d_mixed[:, pl.ds(at, TILE)])
+
+        @pl.when(i < chunks)
+        def _():
+            core_copy(i).start()
+
+        @pl.when((i >= 1) & (i < chunks + 1))
+        def _():
+            j = i - 1
+            core_copy(j).wait()
+            for m in range(chips):
+                a = partial[j % 2, m, core].astype(F32) + theirs[j % DEEP, m].astype(F32)
+                pair[j % 2, m] = a.astype(BF)
+            for m in range(1, chips):
+                chip_copy(j, m).start()
+
+        @pl.when((i >= 2) & (i < chunks + 2))
+        def _():
+            k = i - 2
+            for m in range(1, chips):
+                chip_copy(k, m).wait()
+
+            a = pair[k % 2, chip].astype(F32)
+            for m in range(1, chips):
+                a = a + landed[k % DEEP, m - 1].astype(F32)
+            for way in range(2):
+                @pl.when(sends(way, 1) & (k >= DEEP))
+                def _():
+                    line_copy(way, 1, k - DEEP).wait_send()
+
+            @pl.when(k >= DEEP)
+            def _():
+                own_copy(k - DEEP).wait()
+
+            total[k % DEEP] = a.astype(BF)
+            for way in range(2):
+                @pl.when(sends(way, 1))
+                def _():
+                    line_copy(way, 1, k).start()
+
+            own_copy(k).start()
+
+        for hop in range(2, count + 1):
+            k = i - 2 - LAG * (hop - 1)
+
+            @pl.when((k >= 0) & (k < chunks))
+            def _(k=k, hop=hop):
+                forward(hop, k)
+
+        return carry
+
+    lax.fori_loop(0, chunks + 2 + LAG * (count - 1), step, 0)
+
+    def drain(k, carry):
+        own_copy(k).wait()
+        for way in range(2):
+            for hop in range(1, count):
+                @pl.when(sends(way, hop))
+                def _():
+                    line_copy(way, hop, k).wait_send()
+        return carry
+
+    lax.fori_loop(chunks - DEEP, chunks, drain, 0)
+
+
+def gradients(hid_t, att_t, cot, norm_t, d_gate, d_up, d_mixed, count, shards):
+    chips = shards // 2
+    chunks = cot.shape[1] // TILE + d_gate.shape[1] // HALF + d_mixed.shape[1] // TILE
+    rows = norm_t.shape[0] // shards
+    vmem = pl.BlockSpec(memory_space=pltpu.VMEM)
+    dma = pltpu.SemaphoreType.DMA
+    return pl.pallas_call(
+        gradients_kernel,
+        out_shape=jax.ShapeDtypeStruct((count, chunks, rows, TILE), BF),
+        in_specs=[vmem] * 7,
+        out_specs=pl.BlockSpec(memory_space=pl.ANY),
+        scratch_shapes=[
+            pltpu.VMEM((2, chips, 2, rows, TILE), BF),
+            pltpu.VMEM((DEEP, chips, rows, TILE), BF),
+            pltpu.VMEM((2, chips, rows, TILE), BF),
+            pltpu.VMEM((DEEP, chips - 1, rows, TILE), BF),
+            pltpu.VMEM((DEEP, rows, TILE), BF),
+            dma((2,)),
+            dma((DEEP,)),
+            dma((2, chips - 1)),
+            dma((DEEP, chips - 1)),
+            dma((2, count - 1, DEEP)),
+            dma((2, chunks, count - 1)),
+            dma((DEEP,)),
+        ],
+        compiler_params=pltpu.CompilerParams(
+            collective_id=1, has_side_effects=True, vmem_limit_bytes=50 * 2**20
+        ),
+        cost_estimate=pl.CostEstimate(
+            flops=2 * 2048 * 1024 * TILE * chunks, bytes_accessed=50 * 2**20, transcendentals=0
+        ),
+        name="gradients",
+    )(hid_t, att_t, cot, norm_t, d_gate, d_up, d_mixed)
+
+
+def column_runs(columns, source):
+    out = []
+    for block in range(columns // HALF):
+        first = 0
+        while first < HALF:
+            key, lane = source(block * HALF + first)
+            last = first + 1
+            while last < HALF and source(block * HALF + last) == (key, lane + last - first):
+                last += 1
+            out.append((block, first, last, key, (first - lane) % HALF))
+            first = last
+    return out
+
+
+def assemble_kernel(down_chunks, rows_in, cols_in, qkv_out, gate_out, up_out, down_out, attn_out):
+    count, chunks, rows, _ = rows_in.shape
+    cot_chunks_static = down_chunks
+    ff = gate_out.shape[1]
+    width = qkv_out.shape[1]
+    ff_part = down_out.shape[0] // count
+    attn_part = attn_out.shape[0] // count
+    shards = ff // (count * ff_part)
+    inner_chunks = ff // count // HALF
+    lane = lax.broadcasted_iota(jnp.int32, (rows, HALF), 1)
+
+    def gather(out, runs, load):
+        for block, first, last, key, shift in runs:
+            value = load(key).astype(F32)
+            if shift:
+                value = pltpu.roll(value, shift, 1)
+            if first:
+                value = jnp.where(lane >= first, value, held)
+            held = value
+            if last == HALF:
+                out[:, block * HALF : (block + 1) * HALF] = value
+
+    def inner_source(column):
+        shard, rest = divmod(column, count * ff_part)
+        unit = shard * ff_part + rest % ff_part
+        return (rest // ff_part, unit // HALF), unit % HALF
+
+    def head_source(column):
+        part, rest = divmod(column, width // 3)
+        head, dim = divmod(rest, HD)
+        per = width // 3 // HD // shards // count
+        shard, at = divmod(head, per * count)
+        place, sub = divmod(at, per)
+        local = part * (width // 3 // count) + (shard * per + sub) * HD + dim
+        return (place, local // HALF), local % HALF
+
+    runs = column_runs(ff, inner_source)
+    gather(gate_out, runs, lambda key: rows_in[key[0], cot_chunks_static + key[1], :, :HALF])
+    gather(up_out, runs, lambda key: rows_in[key[0], cot_chunks_static + key[1], :, HALF:])
+    first_head = cot_chunks_static + inner_chunks
+
+    def head_load(key):
+        at = key[1] % 2 * HALF
+        return rows_in[key[0], first_head + key[1] // 2, :, at : at + HALF]
+
+    gather(qkv_out, column_runs(width, head_source), head_load)
+    for p in range(count):
+        down_out[p * ff_part : (p + 1) * ff_part, :] = cols_in[p, 0, :ff_part, :].astype(F32)
+        attn_out[p * attn_part : (p + 1) * attn_part, :] = cols_in[
+            p, 0, ff_part : ff_part + attn_part, :
+        ].astype(F32)
+
+
+def assemble_outputs(pieces, qkv, attn, gate, down):
+    count, chunks, rows, _ = pieces.shape
+    steps = down[1] // TILE
+    part = rows // steps
+    by_rows = lambda shape: pl.BlockSpec((part, shape[1]), lambda i: (i, 0))
+    by_cols = lambda shape: pl.BlockSpec((shape[0], TILE), lambda i: (0, i))
+    return pl.pallas_call(
+        functools.partial(assemble_kernel, steps),
+        grid=(steps,),
+        in_specs=[
+            pl.BlockSpec((count, chunks, part, TILE), lambda i: (0, 0, i, 0)),
+            pl.BlockSpec((count, 1, rows, TILE), lambda i: (0, i, 0, 0)),
+        ],
+        out_specs=[by_rows(qkv), by_rows(gate), by_rows(gate), by_cols(down), by_cols(attn)],
+        out_shape=[jax.ShapeDtypeStruct(s, F32) for s in (qkv, gate, gate, down, attn)],
+        compiler_params=pltpu.CompilerParams(vmem_limit_bytes=40 * 2**20),
+        name="assemble",
+    )(pieces, pieces)
+
+
 def rotation_tables(length):
     half = ROT // 2
     inverse = 10000.0 ** (-jnp.arange(half, dtype=F32) / half)
@@ -233,6 +547,7 @@
     spread = (w_out.shape[0] // HD) % count == 0
     groups = shards if spread else 1
     head_cols = own_heads * HD // groups
+    fast = spread and shards == 8 and ff_part % 16 == 0 and (shards * ff_part) % HALF == 0
 
     def my_cols(w, outer, group, part):
         w = w.reshape(w.shape[0], outer, group, count, part)
@@ -301,7 +616,6 @@
     out = (block.astype(F32) + out).astype(BF)[None]
 
     d_hidden = dot(cot_all, w_hidden, back)
-    grad_down = scatter_rows(dot(hidden, cot_all, over_tokens, BF))
     d_gate_act = (
         d_hidden * up_value * sigmoid_gate * (1.0 + gate_value * (1.0 - sigmoid_gate))
     ).astype(BF)
@@ -310,9 +624,6 @@
     d_attended = dot(cot_all, w_attn, back, BF)
     d_mixed = attend_back(q, k, v, d_attended, attended, lse, tables, own_heads)
     d_mixed = jnp.concatenate(d_mixed, axis=1)
-    grad_inner = scatter_rows(dot(normed, d_inner, over_tokens, BF))
-    grad_attn = dot(attended_low, cot_all, over_tokens, BF)
-    grad_heads = scatter_rows(dot(normed, d_mixed, over_tokens, BF))
 
     d_normed = dot(d_inner, w_inner, back) + dot(d_mixed, w_heads, back)
     small = jnp.stack([jnp.sum(d_normed * x_hat, axis=0), jnp.sum(d_normed, axis=0)])
@@ -332,6 +643,18 @@
     )
     grad_in = (grad_block.astype(F32) + d_input)[None]
 
+    if fast:
+        pieces = gradients(
+            hidden.T, attended_low.T, cot_all, normed.T, d_gate_act, d_up_act, d_mixed, count, shards
+        )
+        heads_all, gate_all, up_all, down_all, attn_all = assemble_outputs(
+            pieces, w_qkv.shape, w_out.shape, w_gate.shape, w_down.shape
+        )
+        return out, grad_in, small[0], small[1], heads_all, attn_all, gate_all, up_all, down_all
+    grad_down = scatter_rows(dot(hidden, cot_all, over_tokens, BF))
+    grad_inner = scatter_rows(dot(normed, d_inner, over_tokens, BF))
+    grad_attn = dot(attended_low, cot_all, over_tokens, BF)
+    grad_heads = scatter_rows(dot(normed, d_mixed, over_tokens, BF))
     down_all = gather_ctx(grad_down).reshape(ff_shard, width).astype(F32)
     if spread:
         attn_all = gather_ctx(scatter_rows(grad_attn)).reshape(w_out.shape).astype(F32)

time: 1080 us -> 918 us (0.85)
  the two profiles are of different devices: /device:TPU:11 before, /device:TPU:0 now
where the time goes in v2:
time: 918 us; the launch traced here: 909 us
  Pallas kernels  303 us (33%)
  local copies, waits for them, and re-layouts  191 us (21%)
  starting transfers between devices  150 us (16%)
  matrix products  104 us (11%)
  blocking collectives  64.6 us (7%)
  waiting for transfers between devices  45 us (5%)
  other arithmetic  42.4 us (5%)
    pallas_call x1, Pallas kernels, gradients(): pl.pallas_call(gradients_kernel, out_shape=jax.ShapeDtypeStruct((count, c...  240 us
    dot_general x9, matrix products, dot(): lax.dot_general(a, b, (dims, ((), ())), preferred_element_type=F32)  104 us
    ppermute x6, starting transfers between devices, line_scatter(): lax.ppermute(to_up.astype(BF), 'ctx', [(count - 1 - i, count - 1 - j) for...  97.6 us
    psum x1, blocking collectives, body(): small = lax.psum(small, ('ctx', 'fsdp'))  47.9 us
    ppermute x6, waiting for transfers between devices, ring_send(): lax.ppermute(value, 'ctx', [(i, (i + steps) % count) for i in range(count)])  44.5 us
    unnamed x99, local copies, waits for them, and re-layouts  37.8 us
    pallas_call x1, Pallas kernels, attend_back(): pl.pallas_call(attend_back_kernel, grid=(heads // 2,), in_specs=[block] *...  33.6 us
    ppermute x6, starting transfers between devices, ring_send(): lax.ppermute(value, 'ctx', [(i, (i + steps) % count) for i in range(count)])  26.2 us
  transfers between devices with their start and end apart: 46, of which 3 were waited for; matrix products, arithmetic and copies ran while one was open for 29% of the time, Pallas kernels for 33%

profile of v2, /device:TPU:0, one launch (start us, length us, event | category | flops | bytes accessed | tf_op | source)
XLA Modules:
  0.0 908.6 jit_solution(1976901078508517907)
XLA Ops:
  0.7 2.4 copy.89
  3.1 3.0 collective-permute-start
  6.1 2.6 collective-permute-start.1
  10.0 4.5 copy.92
  14.6 4.5 copy.91
  22.4 2.4 collective-permute-start.3
  27.3 4.6 copy.90
  32.1 2.5 copy.105
  36.5 5.1 broadcast_in_dim.155
  53.5 8.0 all-gather
  61.5 8.8 all-gather.1
  87.5 16.5 %collective-permute-start.37 = (bf16[256,2048]{0,1:T(8,128)(2,1)}, bf16[256,2048]{0,1:T(8,128)(2,1)}, u32[]{:S(2)}, u32[]{:S(2)}) collective-permute-start(bf16[256,2048]{0,1:T(8,128)(2,1)} %bitcast.59), channel_id=1, source_target_pairs={{0,8},{8,16},{16,24},{24,0},{1,9},{9,17},{17,25},{25,1},{2,10},{10... | collective-permute-start | bytes 3145736 | tf_op jit(solution)/shard_map/ppermute | solution.py:28
  114.4 2.6 collective-permute-start.39
  123.3 4.7 collective-permute-done.37
  128.5 39.8 %collective-permute-done.38 = bf16[256,2048]{0,1:T(8,128)(2,1)} collective-permute-done((bf16[256,2048]{0,1:T(8,128)(2,1)}, bf16[256,2048]{0,1:T(8,128)(2,1)}, u32[]{:S(2)}, u32[]{:S(2)}) %collective-permute-start.38) | collective-permute-done | bytes 1048608 | tf_op jit(solution)/shard_map/ppermute | solution.py:28
  168.3 2.4 collective-permute-start.9
  170.8 3.2 broadcast_in_dim.135
  178.3 2.3 constant_dynamic-update-slice_fusion.2
  181.2 2.3 constant_dynamic-update-slice_fusion.1
  183.5 2.3 constant_dynamic-update-slice_fusion
  185.8 6.5 copy.123.cot
  192.4 2.3 copy.94
  197.6 2.3 copy.97
  199.9 2.3 copy.99
  206.4 3.3 broadcast_in_dim.164
  213.2 2.5 copy.108
  217.2 2.5 copy.110
  219.7 2.9 copy.112
  222.7 2.7 constant_dynamic-update-slice_fusion.8
  230.4 12.6 %fusion.10 = f32[1024,1408]{1,0:T(8,128)} fusion(bf16[2048,2816]{1,0:T(8,128)(2,1)} %bitcast.130, bf16[1024,2048]{0,1:T(8,128)(2,1)S(1)} %copy-done.16, f32[2048]{0:T(1024)S(1)} %bitcast.150, f32[2048]{0:T(1024)S(1)} %bitcast.145, f32[1024]{0:T(1024)S(1)} %add_rsqrt_fusion, f32[1024]{0:T(1024)S(1)} %broadcast_multiply_fusion), kind=kOutput, calls=%fused_computation.12 | convolution fusion | flops 5918162944 | bytes 15753216 | tf_op jit(solution)/shard_map/dot_general | solution.py:36
  243.0 10.1 %fusion.8 = f32[1024,1408]{1,0:T(8,128)} fusion(bf16[2048,2816]{1,0:T(8,128)(2,1)S(1)} %bitcast.132, bf16[1024,2048]{0,1:T(8,128)(2,1)S(1)} %copy-done.16, f32[2048]{0:T(1024)S(1)} %bitcast.151, f32[2048]{0:T(1024)S(1)} %bitcast.146, f32[1024]{0:T(1024)S(1)} %add_rsqrt_fusion, f32[1024]{0:T(1024)S(1)} %broadcast_multiply_fusion), kind=kOutput, calls=%fused_computation.10 | convolution fusion | flops 5918162944 | bytes 15753216 | tf_op jit(solution)/shard_map/dot_general | solution.py:36
  253.1 6.4 copy.122
  259.5 6.3 copy.121
  275.8 2.3 copy.98
  278.1 2.5 collective-permute-start.17
  291.1 12.1 %fusion.45.mq.mk.mv = f32[1024,1536]{1,0:T(8,128)} fusion(bf16[2048,1536]{1,0:T(8,128)(2,1)} %bitcast.21, bf16[1024,2048]{0,1:T(8,128)(2,1)S(1)} %copy-done.17, f32[2048]{0:T(1024)S(1)} %bitcast.152, f32[2048]{0:T(1024)S(1)} %bitcast.147, f32[1024]{0:T(1024)S(1)} %add_rsqrt_fusion, f32[1024]{0:T(1024)S(1)} %broadcast_multiply_fusion), kind=kOutput, calls=%fused_computation.143 | convolution fusion | flops 6455033856 | bytes 16801792 | tf_op jit(solution)/shard_map/dot_general | solution.py:36
  303.2 19.5 %attend.1 = (bf16[1024,512]{1,0:T(8,128)(2,1)S(1)}, bf16[1024,512]{1,0:T(8,128)(2,1)S(1)}, bf16[1024,512]{1,0:T(8,128)(2,1)S(1)}, f32[1024,512]{1,0:T(8,128)S(1)}, f32[1024,512]{1,0:T(8,128)S(1)}) custom-call(f32[1024,1536]{1,0:T(8,128)} %fusion.45.mq.mk.mv, f32[1024,1536]{1,0:T(8,128)} %fusion.45.mq.mk.mv, f32[1024,1536]{1,0:T(8,128)} %fusion.45.mq.mk.mv, ...), custom_call_target="tpu_custom_call" | custom-call | flops 4294967296 | bytes 13631488 | tf_op jit(solution)/shard_map/attend/pallas_call | solution.py:139
  340.6 5.4 convolution_convert_fusion.do_in
  346.1 33.6 %attend_back.1 = (bf16[1024,512]{1,0:T(8,128)(2,1)S(1)}, bf16[1024,512]{1,0:T(8,128)(2,1)S(1)}, bf16[1024,512]{1,0:T(8,128)(2,1)S(1)}) custom-call(bf16[1024,512]{1,0:T(8,128)(2,1)S(1)} %copy-done.10, bf16[1024,512]{1,0:T(8,128)(2,1)S(1)} %copy-done.12, bf16[1024,512]{1,0:T(8,128)(2,1)S(1)} %copy-done.14, ...), custom_call_target="tpu_custom_call" | custom-call | flops 10737418240 | bytes 11534336 | tf_op jit(solution)/shard_map/attend_back/pallas_call | solution.py:190
  380.0 11.9 %fusion.49 = f32[1024,2048]{0,1:T(8,128)} fusion(bf16[1024,1536]{1,0:T(8,128)(2,1)S(1)} %constant_dynamic-update-slice_fusion.24.d_mixed, bf16[2048,1536]{1,0:T(8,128)(2,1)} %bitcast.21), kind=kOutput, calls=%fused_computation.146 | convolution fusion | flops 6442450944 | bytes 17825792 | tf_op jit(solution)/shard_map/dot_general | solution.py:36
  392.9 2.6 bitcast_dynamic-update-slice_fusion.3
  400.5 13.5 %multiply_convert_fusion.1 = (bf16[1024,1408]{1,0:T(8,128)(2,1)}, bf16[1024,1408]{1,0:T(8,128)(2,1)}) fusion(f32[1024,1408]{1,0:T(8,128)S(1)} %bitcast.136, f32[1024,1408]{1,0:T(8,128)} %fusion.8, bf16[1024,2048]{0,1:T(8,128)(2,1)S(1)} %copy-done.24, bf16[1408,2048]{1,0:T(8,128)(2,1)} %bitcast.51), kind=kOutput, calls=%fused_computation.26 | convolution fusion | flops 5924323328 | bytes 27262976 | tf_op jit(solution)/shard_map/dot_general | solution.py:36
  414.0 12.6 %fusion.23 = f32[1024,2048]{0,1:T(8,128)} fusion(bf16[1408,2048]{1,0:T(8,128)(2,1)} %bitcast.51, f32[1024,1408]{1,0:T(8,128)} %fusion.8, f32[1024,1408]{1,0:T(8,128)S(1)} %bitcast.136), kind=kOutput, calls=%fused_computation.34 | convolution fusion | flops 5914230784 | bytes 25690112 | tf_op jit(solution)/shard_map/dot_general | solution.py:36
  426.6 19.8 %fusion.20 = f32[1024,2048]{0,1:T(8,128)} fusion(f32[1024,2048]{0,1:T(8,128)} %fusion.49, bf16[2048,2816]{1,0:T(8,128)(2,1)} %bitcast.131, bf16[1024,1408]{1,0:T(8,128)(2,1)} %get-tuple-element.85.d_up, bf16[1024,1408]{1,0:T(8,128)(2,1)} %get-tuple-element.84.d_gate), kind=kOutput, calls=%fused_computation.29 | convolution fusion | flops 11824791552 | bytes 34078720 | tf_op jit(solution)/shard_map/dot_general | solution.py:36
  446.4 3.4 dynamic-slice_convert_fusion.1
  450.5 26.3 %collective-permute-start.43 = (bf16[256,2048]{0,1:T(8,128)(2,1)}, bf16[256,2048]{0,1:T(8,128)(2,1)S(1)}, u32[]{:S(2)}, u32[]{:S(2)}) collective-permute-start(bf16[256,2048]{0,1:T(8,128)(2,1)} %get-tuple-element.89), channel_id=1, source_target_pairs={{0,8},{1,9},{2,10},{3,11},{4,12},{5,13},{6,14},{7,15}} | collective-permute-start | bytes 3145736 | tf_op jit(solution)/shard_map/ppermute | solution.py:94
  476.8 6.4 convolution_add_fusion
  486.9 2.8 add_convert_fusion.3
  491.4 4.6 fusion.16.hid_t
  501.3 3.3 add_convert_fusion.2
  504.7 32.0 %collective-permute-start.44 = (bf16[256,2048]{0,1:T(8,128)(2,1)S(1)}, bf16[256,2048]{0,1:T(8,128)(2,1)S(1)}, u32[]{:S(2)}, u32[]{:S(2)}) collective-permute-start(bf16[256,2048]{0,1:T(8,128)(2,1)S(1)} %get-tuple-element.87), channel_id=1, source_target_pairs={{8,16},{0,8},{9,17},{1,9},{10,18},{2,10},{11,19},{3,11},{12,20},{4... | collective-permute-start | bytes 3145736 | tf_op jit(solution)/shard_map/ppermute | solution.py:94
  536.7 6.3 fusion.6
  546.5 19.8 %collective-permute-start.35 = (bf16[256,2048]{0,1:T(8,128)(2,1)}, bf16[256,2048]{0,1:T(8,128)(2,1)}, u32[]{:S(2)}, u32[]{:S(2)}) collective-permute-start(bf16[256,2048]{0,1:T(8,128)(2,1)} %get-tuple-element.91), channel_id=1, source_target_pairs={{8,16},{0,8},{9,17},{1,9},{10,18},{2,10},{11,19},{3,11},{12,20},{4... | collective-permute-start | bytes 3145736 | tf_op jit(solution)/shard_map/ppermute | solution.py:94
  566.4 2.9 add_convert_fusion
  569.2 12.4 %collective-permute-start.45 = (bf16[256,2048]{0,1:T(8,128)(2,1)}, bf16[256,2048]{0,1:T(8,128)(2,1)}, u32[]{:S(2)}, u32[]{:S(2)}) collective-permute-start(bf16[256,2048]{0,1:T(8,128)(2,1)} %add_convert_fusion), channel_id=1, source_target_pairs={{16,24},{8,16},{0,8},{17,25},{9,17},{1,9},{18,26},{10,18},{2,10},{... | collective-permute-start | bytes 3145736 | tf_op jit(solution)/shard_map/ppermute | solution.py:94
  581.6 239.7 %gradients.1.rows_in.cols_in = bf16[4,25,256,256]{3,2,1,0:T(8,128)(2,1)} custom-call(bf16[1408,1024]{1,0:T(8,128)(2,1)S(1)} %fusion.16.hid_t, bf16[512,1024]{1,0:T(8,128)(2,1)S(1)} %bitcast.124, bf16[1024,2048]{1,0:T(8,128)(2,1)} %copy.123.cot, bf16[2048,1024]{1,0:T(8,128)(2,1)} %get-tuple-element.94.norm_t, bf16[1024,1408]{1,0:T(8,128)(2,1)} %get-tuple-element.84.d_gate, ...), custom_call_target="tpu_custom_call" | custom-call | flops 26843545600 | bytes 52428800 | tf_op jit(solution)/shard_map/gradients/pallas_call | solution.py:405
  821.3 4.7 copy-done.2
  826.0 10.2 %assemble.1 = (f32[256,6144]{1,0:T(8,128)}, f32[256,5632]{1,0:T(8,128)}, f32[256,5632]{1,0:T(8,128)}, f32[704,2048]{1,0:T(8,128)}, f32[256,2048]{1,0:T(8,128)}) custom-call(bf16[4,25,256,256]{3,2,1,0:T(8,128)(2,1)S(1)} %copy-done.2, bf16[4,25,256,256]{3,2,1,0:T(8,128)(2,1)S(1)} %copy-done.2), custom_call_target="tpu_custom_call" | custom-call | tf_op jit(solution)/shard_map/assemble/pallas_call | solution.py:507
  837.6 2.6 add_convert_fusion.4
  840.2 5.5 collective-permute-start.36
  845.7 47.9 %psum.7 = f32[2,2048]{1,0:T(2,128)S(1)} all-reduce(f32[2,2048]{1,0:T(2,128)S(1)} %pad_maximum_fusion.1), channel_id=1, replica_groups=mesh['ctx'=4,'fsdp'=8] {'ctx','fsdp'}, use_global_device_ids=true, to_apply=%region_8.9 | all-reduce | flops 4096 | bytes 32768 | tf_op jit(solution)/shard_map/psum | solution.py:630
  894.2 3.0 fusion.47
  897.3 5.8 fusion.33
  905.3 2.9 copy.125
  (259 shorter events, 134.3 us)
Async XLA Ops:
  0.6 81.8 %copy-start = (bf16[704,2048]{1,0:T(8,128)(2,1)S(1)}, bf16[704,2048]{1,0:T(8,128)(2,1)}, u32[]{:S(2)}) copy-start(bf16[704,2048]{1,0:T(8,128)(2,1)} %param.18) | copy-start | bytes 8650756
  3.1 81.6 %collective-permute-start = (bf16[256,2048]{0,1:T(8,128)(2,1)}, bf16[256,2048]{0,1:T(8,128)(2,1)}, u32[]{:S(2)}, u32[]{:S(2)}) collective-permute-start(bf16[256,2048]{0,1:T(8,128)(2,1)} %bitcast.125), channel_id=1, source_target_pairs={{0,8},{8,16},{16,24},{24,0},{1,9},{9,17},{17,25},{25,1},{2,10},{10... | collective-permute-start | bytes 3145736 | tf_op jit(solution)/shard_map/ppermute | solution.py:28
  6.1 81.4 %collective-permute-start.1 = (bf16[256,2048]{0,1:T(8,128)(2,1)}, bf16[256,2048]{0,1:T(8,128)(2,1)}, u32[]{:S(2)}, u32[]{:S(2)}) collective-permute-start(bf16[256,2048]{0,1:T(8,128)(2,1)} %bitcast.126), channel_id=1, source_target_pairs={{0,16},{8,24},{16,0},{24,8},{1,17},{9,25},{17,1},{25,9},{2,18},{10... | collective-permute-start | bytes 3145736 | tf_op jit(solution)/shard_map/ppermute | solution.py:28
  8.7 75.4 %collective-permute-start.2 = (bf16[256,2048]{0,1:T(8,128)(2,1)}, bf16[256,2048]{0,1:T(8,128)(2,1)}, u32[]{:S(2)}, u32[]{:S(2)}) collective-permute-start(bf16[256,2048]{0,1:T(8,128)(2,1)} %bitcast.127), channel_id=1, source_target_pairs={{0,24},{8,0},{16,8},{24,16},{1,25},{9,1},{17,9},{25,17},{2,26},{10... | collective-permute-start | bytes 3145736 | tf_op jit(solution)/shard_map/ppermute | solution.py:28
  22.4 92.0 %collective-permute-start.3 = (bf16[256,2816]{0,1:T(8,128)(2,1)}, bf16[256,2816]{0,1:T(8,128)(2,1)}, u32[]{:S(2)}, u32[]{:S(2)}) collective-permute-start(bf16[256,2816]{0,1:T(8,128)(2,1)} %get-tuple-element.96), channel_id=1, source_target_pairs={{0,6},{1,7},{2,4},{3,5},{4,2},{5,3},{6,0},{7,1},{8,14},{9,15},{10,... | collective-permute-start | bytes 4325384 | tf_op jit(solution)/shard_map/ppermute | solution.py:23
  24.8 83.9 %collective-permute-start.19 = (bf16[256,2816]{0,1:T(8,128)(2,1)}, bf16[256,2816]{0,1:T(8,128)(2,1)}, u32[]{:S(2)}, u32[]{:S(2)}) collective-permute-start(bf16[256,2816]{0,1:T(8,128)(2,1)} %get-tuple-element.96), channel_id=1, source_target_pairs={{0,1},{1,0},{2,3},{3,2},{4,5},{5,4},{6,7},{7,6},{8,9},{9,8},{10,11... | collective-permute-start | bytes 4325384 | tf_op jit(solution)/shard_map/ppermute | solution.py:23
  36.5 17.0 %copy-start.38 = (bf16[256]{0:T(256)(128)(2,1)S(1)}, bf16[256]{0:T(256)(128)(2,1)}, u32[]{:S(2)}) copy-start(bf16[256]{0:T(256)(128)(2,1)} %param.12) | copy-start | bytes 1540
  36.5 25.0 %copy-start.39 = (bf16[256]{0:T(256)(128)(2,1)S(1)}, bf16[256]{0:T(256)(128)(2,1)}, u32[]{:S(2)}) copy-start(bf16[256]{0:T(256)(128)(2,1)} %param.13) | copy-start | bytes 1540
  84.1 35.6 %collective-permute-start.20 = (bf16[256,2816]{0,1:T(8,128)(2,1)}, bf16[256,2816]{0,1:T(8,128)(2,1)}, u32[]{:S(2)}, u32[]{:S(2)}) collective-permute-start(bf16[256,2816]{0,1:T(8,128)(2,1)} %get-tuple-element.96), channel_id=1, source_target_pairs={{0,2},{1,3},{2,0},{3,1},{4,6},{5,7},{6,4},{7,5},{8,10},{9,11},{10,... | collective-permute-start | bytes 4325384 | tf_op jit(solution)/shard_map/ppermute | solution.py:23
  84.7 36.7 %collective-permute-start.22 = (bf16[256,2816]{0,1:T(8,128)(2,1)}, bf16[256,2816]{0,1:T(8,128)(2,1)}, u32[]{:S(2)}, u32[]{:S(2)}) collective-permute-start(bf16[256,2816]{0,1:T(8,128)(2,1)} %get-tuple-element.96), channel_id=1, source_target_pairs={{0,4},{1,5},{2,6},{3,7},{4,0},{5,1},{6,2},{7,3},{8,12},{9,13},{10,... | collective-permute-start | bytes 4325384 | tf_op jit(solution)/shard_map/ppermute | solution.py:23
  87.5 40.5 %collective-permute-start.37 = (bf16[256,2048]{0,1:T(8,128)(2,1)}, bf16[256,2048]{0,1:T(8,128)(2,1)}, u32[]{:S(2)}, u32[]{:S(2)}) collective-permute-start(bf16[256,2048]{0,1:T(8,128)(2,1)} %bitcast.59), channel_id=1, source_target_pairs={{0,8},{8,16},{16,24},{24,0},{1,9},{9,17},{17,25},{25,1},{2,10},{10... | collective-permute-start | bytes 3145736 | tf_op jit(solution)/shard_map/ppermute | solution.py:28
  108.7 59.6 %collective-permute-start.38 = (bf16[256,2048]{0,1:T(8,128)(2,1)}, bf16[256,2048]{0,1:T(8,128)(2,1)}, u32[]{:S(2)}, u32[]{:S(2)}) collective-permute-start(bf16[256,2048]{0,1:T(8,128)(2,1)} %bitcast.59), channel_id=1, source_target_pairs={{0,16},{8,24},{16,0},{24,8},{1,17},{9,25},{17,1},{25,9},{2,18},{10... | collective-permute-start | bytes 3145736 | tf_op jit(solution)/shard_map/ppermute | solution.py:28
  114.4 66.2 %collective-permute-start.39 = (bf16[256,2048]{0,1:T(8,128)(2,1)}, bf16[256,2048]{0,1:T(8,128)(2,1)}, u32[]{:S(2)}, u32[]{:S(2)}) collective-permute-start(bf16[256,2048]{0,1:T(8,128)(2,1)} %bitcast.59), channel_id=1, source_target_pairs={{0,24},{8,0},{16,8},{24,16},{1,25},{9,1},{17,9},{25,17},{2,26},{10... | collective-permute-start | bytes 3145736 | tf_op jit(solution)/shard_map/ppermute | solution.py:28
  119.7 61.0 %collective-permute-start.4 = (bf16[256,1536]{0,1:T(8,128)(2,1)}, bf16[256,1536]{0,1:T(8,128)(2,1)}, u32[]{:S(2)}, u32[]{:S(2)}) collective-permute-start(bf16[256,1536]{0,1:T(8,128)(2,1)} %bitcast.8), channel_id=1, source_target_pairs={{0,1},{1,0},{2,3},{3,2},{4,5},{5,4},{6,7},{7,6},{8,9},{9,8},{10,11... | collective-permute-start | bytes 2359304 | tf_op jit(solution)/shard_map/ppermute | solution.py:23
  121.4 59.7 %collective-permute-start.5 = (bf16[256,1536]{0,1:T(8,128)(2,1)}, bf16[256,1536]{0,1:T(8,128)(2,1)}, u32[]{:S(2)}, u32[]{:S(2)}) collective-permute-start(bf16[256,1536]{0,1:T(8,128)(2,1)} %bitcast.8), channel_id=1, source_target_pairs={{0,2},{1,3},{2,0},{3,1},{4,6},{5,7},{6,4},{7,5},{8,10},{9,11},{10,... | collective-permute-start | bytes 2359304 | tf_op jit(solution)/shard_map/ppermute | solution.py:23
  128.0 69.4 %collective-permute-start.7 = (bf16[256,1536]{0,1:T(8,128)(2,1)}, bf16[256,1536]{0,1:T(8,128)(2,1)}, u32[]{:S(2)}, u32[]{:S(2)}) collective-permute-start(bf16[256,1536]{0,1:T(8,128)(2,1)} %bitcast.8), channel_id=1, source_target_pairs={{0,4},{1,5},{2,6},{3,7},{4,0},{5,1},{6,2},{7,3},{8,12},{9,13},{10,... | collective-permute-start | bytes 2359304 | tf_op jit(solution)/shard_map/ppermute | solution.py:23
  168.3 28.6 %collective-permute-start.9 = (bf16[256,1536]{0,1:T(8,128)(2,1)}, bf16[256,1536]{0,1:T(8,128)(2,1)}, u32[]{:S(2)}, u32[]{:S(2)}) collective-permute-start(bf16[256,1536]{0,1:T(8,128)(2,1)} %bitcast.8), channel_id=1, source_target_pairs={{0,6},{1,7},{2,4},{3,5},{4,2},{5,3},{6,0},{7,1},{8,14},{9,15},{10,... | collective-permute-start | bytes 2359304 | tf_op jit(solution)/shard_map/ppermute | solution.py:23
  180.6 31.1 %collective-permute-start.21 = (bf16[256,2816]{0,1:T(8,128)(2,1)}, bf16[256,2816]{0,1:T(8,128)(2,1)}, u32[]{:S(2)}, u32[]{:S(2)}) collective-permute-start(bf16[256,2816]{0,1:T(8,128)(2,1)} %collective-permute-done.20), channel_id=1, source_target_pairs={{0,1},{1,0},{2,3},{3,2},{4,5},{5,4},{6,7},{7,6},{8,9},{9,8},{10,11... | collective-permute-start | bytes 4325384 | tf_op jit(solution)/shard_map/ppermute | solution.py:23
  180.6 35.1 %collective-permute-start.23 = (bf16[256,2816]{0,1:T(8,128)(2,1)}, bf16[256,2816]{0,1:T(8,128)(2,1)}, u32[]{:S(2)}, u32[]{:S(2)}) collective-permute-start(bf16[256,2816]{0,1:T(8,128)(2,1)} %collective-permute-done.22), channel_id=1, source_target_pairs={{0,1},{1,0},{2,3},{3,2},{4,5},{5,4},{6,7},{7,6},{8,9},{9,8},{10,11... | collective-permute-start | bytes 4325384 | tf_op jit(solution)/shard_map/ppermute | solution.py:23
  181.1 38.6 %collective-permute-start.24 = (bf16[256,2816]{0,1:T(8,128)(2,1)}, bf16[256,2816]{0,1:T(8,128)(2,1)}, u32[]{:S(2)}, u32[]{:S(2)}) collective-permute-start(bf16[256,2816]{0,1:T(8,128)(2,1)} %collective-permute-done.3), channel_id=1, source_target_pairs={{0,1},{1,0},{2,3},{3,2},{4,5},{5,4},{6,7},{7,6},{8,9},{9,8},{10,11... | collective-permute-start | bytes 4325384 | tf_op jit(solution)/shard_map/ppermute | solution.py:23
  196.9 68.8 %collective-permute-start.11 = (bf16[176,2048]{1,0:T(8,128)(2,1)}, bf16[176,2048]{1,0:T(8,128)(2,1)}, u32[]{:S(2)}, u32[]{:S(2)}) collective-permute-start(bf16[176,2048]{1,0:T(8,128)(2,1)} %constant_dynamic-slice_fusion.7), channel_id=1, source_target_pairs={{0,6},{1,7},{2,4},{3,5},{4,2},{5,3},{6,0},{7,1},{8,14},{9,15},{10,... | collective-permute-start | bytes 2162696 | tf_op jit(solution)/shard_map/ppermute | solution.py:23
  197.4 68.9 %collective-permute-start.25 = (bf16[176,2048]{1,0:T(8,128)(2,1)}, bf16[176,2048]{1,0:T(8,128)(2,1)}, u32[]{:S(2)}, u32[]{:S(2)}) collective-permute-start(bf16[176,2048]{1,0:T(8,128)(2,1)} %constant_dynamic-slice_fusion.7), channel_id=1, source_target_pairs={{0,1},{1,0},{2,3},{3,2},{4,5},{5,4},{6,7},{7,6},{8,9},{9,8},{10,11... | collective-permute-start | bytes 2162696 | tf_op jit(solution)/shard_map/ppermute | solution.py:23
  211.7 58.1 %collective-permute-start.26 = (bf16[176,2048]{1,0:T(8,128)(2,1)}, bf16[176,2048]{1,0:T(8,128)(2,1)}, u32[]{:S(2)}, u32[]{:S(2)}) collective-permute-start(bf16[176,2048]{1,0:T(8,128)(2,1)} %constant_dynamic-slice_fusion.7), channel_id=1, source_target_pairs={{0,2},{1,3},{2,0},{3,1},{4,6},{5,7},{6,4},{7,5},{8,10},{9,11},{10,... | collective-permute-start | bytes 2162696 | tf_op jit(solution)/shard_map/ppermute | solution.py:23
  215.7 118.4 %collective-permute-start.28 = (bf16[176,2048]{1,0:T(8,128)(2,1)}, bf16[176,2048]{1,0:T(8,128)(2,1)}, u32[]{:S(2)}, u32[]{:S(2)}) collective-permute-start(bf16[176,2048]{1,0:T(8,128)(2,1)} %constant_dynamic-slice_fusion.7), channel_id=1, source_target_pairs={{0,4},{1,5},{2,6},{3,7},{4,0},{5,1},{6,2},{7,3},{8,12},{9,13},{10,... | collective-permute-start | bytes 2162696 | tf_op jit(solution)/shard_map/ppermute | solution.py:23
  219.7 52.8 %collective-permute-start.6 = (bf16[256,1536]{0,1:T(8,128)(2,1)}, bf16[256,1536]{0,1:T(8,128)(2,1)}, u32[]{:S(2)}, u32[]{:S(2)}) collective-permute-start(bf16[256,1536]{0,1:T(8,128)(2,1)} %collective-permute-done.5), channel_id=1, source_target_pairs={{0,1},{1,0},{2,3},{3,2},{4,5},{5,4},{6,7},{7,6},{8,9},{9,8},{10,11... | collective-permute-start | bytes 2359304 | tf_op jit(solution)/shard_map/ppermute | solution.py:23
  230.4 12.6 %copy-start.25 = (bf16[8,256,2816]{2,1,0:T(8,128)(2,1)S(1)}, bf16[8,256,2816]{2,1,0:T(8,128)(2,1)}, u32[]{:S(2)}) copy-start(bf16[8,256,2816]{2,1,0:T(8,128)(2,1)} %constant_dynamic-update-slice_fusion.4) | copy-start | bytes 34603012
  265.8 9.6 %collective-permute-start.8 = (bf16[256,1536]{0,1:T(8,128)(2,1)}, bf16[256,1536]{0,1:T(8,128)(2,1)}, u32[]{:S(2)}, u32[]{:S(2)}) collective-permute-start(bf16[256,1536]{0,1:T(8,128)(2,1)} %collective-permute-done.7), channel_id=1, source_target_pairs={{0,1},{1,0},{2,3},{3,2},{4,5},{5,4},{6,7},{7,6},{8,9},{9,8},{10,11... | collective-permute-start | bytes 2359304 | tf_op jit(solution)/shard_map/ppermute | solution.py:23
  266.4 11.8 %collective-permute-start.10 = (bf16[256,1536]{0,1:T(8,128)(2,1)}, bf16[256,1536]{0,1:T(8,128)(2,1)}, u32[]{:S(2)}, u32[]{:S(2)}) collective-permute-start(bf16[256,1536]{0,1:T(8,128)(2,1)} %collective-permute-done.9), channel_id=1, source_target_pairs={{0,1},{1,0},{2,3},{3,2},{4,5},{5,4},{6,7},{7,6},{8,9},{9,8},{10,11... | collective-permute-start | bytes 2359304 | tf_op jit(solution)/shard_map/ppermute | solution.py:23
  268.7 20.6 %copy-start.30 = (bf16[1,256,1536]{2,1,0:T(8,128)(2,1)S(1)}, bf16[1,256,1536]{2,1,0:T(8,128)(2,1)}, u32[]{:S(2)}) copy-start(bf16[1,256,1536]{2,1,0:T(8,128)(2,1)} %copy.99) | copy-start | bytes 2359300
  269.8 20.4 %copy-start.26 = (bf16[8,64,2048]{2,1,0:T(8,128)(2,1)}, bf16[8,64,2048]{2,1,0:T(8,128)(2,1)S(1)}, u32[]{:S(2)}) copy-start(bf16[8,64,2048]{2,1,0:T(8,128)(2,1)S(1)} %bitcast_dynamic-update-slice_fusion.15) | copy-start | bytes 6291460
  269.8 60.4 %collective-permute-start.12 = (bf16[64,2048]{1,0:T(8,128)(2,1)}, bf16[64,2048]{1,0:T(8,128)(2,1)}, u32[]{:S(2)}, u32[]{:S(2)}) collective-permute-start(bf16[64,2048]{1,0:T(8,128)(2,1)} %constant_dynamic-slice_fusion.8), channel_id=1, source_target_pairs={{0,1},{1,0},{2,3},{3,2},{4,5},{5,4},{6,7},{7,6},{8,9},{9,8},{10,11... | collective-permute-start | bytes 786440 | tf_op jit(solution)/shard_map/ppermute | solution.py:23
  272.5 57.7 %collective-permute-start.13 = (bf16[64,2048]{1,0:T(8,128)(2,1)}, bf16[64,2048]{1,0:T(8,128)(2,1)}, u32[]{:S(2)}, u32[]{:S(2)}) collective-permute-start(bf16[64,2048]{1,0:T(8,128)(2,1)} %constant_dynamic-slice_fusion.8), channel_id=1, source_target_pairs={{0,2},{1,3},{2,0},{3,1},{4,6},{5,7},{6,4},{7,5},{8,10},{9,11},{10,... | collective-permute-start | bytes 786440 | tf_op jit(solution)/shard_map/ppermute | solution.py:23
  275.3 58.8 %collective-permute-start.15 = (bf16[64,2048]{1,0:T(8,128)(2,1)}, bf16[64,2048]{1,0:T(8,128)(2,1)}, u32[]{:S(2)}, u32[]{:S(2)}) collective-permute-start(bf16[64,2048]{1,0:T(8,128)(2,1)} %constant_dynamic-slice_fusion.8), channel_id=1, source_target_pairs={{0,4},{1,5},{2,6},{3,7},{4,0},{5,1},{6,2},{7,3},{8,12},{9,13},{10,... | collective-permute-start | bytes 786440 | tf_op jit(solution)/shard_map/ppermute | solution.py:23
  278.1 56.5 %collective-permute-start.17 = (bf16[64,2048]{1,0:T(8,128)(2,1)}, bf16[64,2048]{1,0:T(8,128)(2,1)}, u32[]{:S(2)}, u32[]{:S(2)}) collective-permute-start(bf16[64,2048]{1,0:T(8,128)(2,1)} %constant_dynamic-slice_fusion.8), channel_id=1, source_target_pairs={{0,6},{1,7},{2,4},{3,5},{4,2},{5,3},{6,0},{7,1},{8,14},{9,15},{10,... | collective-permute-start | bytes 786440 | tf_op jit(solution)/shard_map/ppermute | solution.py:23
  291.1 12.1 %copy-start.3 = (f32[1024,128]{1,0:T(8,128)S(1)}, f32[1024,128]{1,0:T(8,128)}, u32[]{:S(2)}) copy-start(f32[1024,128]{1,0:T(8,128)} %copy.102.first) | copy-start | bytes 1572868
  291.1 12.1 %copy-start.4 = (f32[1024,128]{1,0:T(8,128)S(1)}, f32[1024,128]{1,0:T(8,128)}, u32[]{:S(2)}) copy-start(f32[1024,128]{1,0:T(8,128)} %copy.103.second) | copy-start | bytes 1572868
  330.2 61.8 %collective-permute-start.27 = (bf16[176,2048]{1,0:T(8,128)(2,1)}, bf16[176,2048]{1,0:T(8,128)(2,1)S(1)}, u32[]{:S(2)}, u32[]{:S(2)}) collective-permute-start(bf16[176,2048]{1,0:T(8,128)(2,1)} %collective-permute-done.26), channel_id=1, source_target_pairs={{0,1},{1,0},{2,3},{3,2},{4,5},{5,4},{6,7},{7,6},{8,9},{9,8},{10,11... | collective-permute-start | bytes 2162696 | tf_op jit(solution)/shard_map/ppermute | solution.py:23
  330.3 4.4 collective-permute-start.14
  334.1 65.5 %collective-permute-start.30 = (bf16[176,2048]{1,0:T(8,128)(2,1)}, bf16[176,2048]{1,0:T(8,128)(2,1)S(1)}, u32[]{:S(2)}, u32[]{:S(2)}) collective-permute-start(bf16[176,2048]{1,0:T(8,128)(2,1)} %collective-permute-done.11), channel_id=1, source_target_pairs={{0,1},{1,0},{2,3},{3,2},{4,5},{5,4},{6,7},{7,6},{8,9},{9,8},{10,11... | collective-permute-start | bytes 2162696 | tf_op jit(solution)/shard_map/ppermute | solution.py:23
  334.2 61.3 %collective-permute-start.29 = (bf16[176,2048]{1,0:T(8,128)(2,1)}, bf16[176,2048]{1,0:T(8,128)(2,1)}, u32[]{:S(2)}, u32[]{:S(2)}) collective-permute-start(bf16[176,2048]{1,0:T(8,128)(2,1)} %collective-permute-done.28), channel_id=1, source_target_pairs={{0,1},{1,0},{2,3},{3,2},{4,5},{5,4},{6,7},{7,6},{8,9},{9,8},{10,11... | collective-permute-start | bytes 2162696 | tf_op jit(solution)/shard_map/ppermute | solution.py:23
  334.6 2.9 collective-permute-start.16
  334.7 5.2 collective-permute-start.18
  379.9 20.6 %slice-start.2 = ((s8[5767168]{0:T(1024)(128)(4,1)}), s8[4194304]{0:T(1024)(128)(4,1)S(1)}, s32[]{:S(2)}) async-start(s8[5767168]{0:T(1024)(128)(4,1)} %bitcast.135), calls=%async_computation.2 | async-start | bytes 8388608
  380.0 11.9 %copy-start.33 = (bf16[1024,1536]{1,0:T(8,128)(2,1)}, bf16[1024,1536]{1,0:T(8,128)(2,1)S(1)}, u32[]{:S(2)}) copy-start(bf16[1024,1536]{1,0:T(8,128)(2,1)S(1)} %constant_dynamic-update-slice_fusion.24.d_mixed) | copy-start | bytes 9437188
  380.0 20.5 %slice-start.3 = ((s8[5767168]{0:T(1024)(128)(4,1)}), s8[1572864]{0:T(1024)(128)(4,1)S(1)}, s32[]{:S(2)}) async-start(s8[5767168]{0:T(1024)(128)(4,1)} %bitcast.135), calls=%async_computation.3 | async-start | bytes 3145728
  449.8 37.1 %collective-permute-start.40 = (bf16[256,2048]{0,1:T(8,128)(2,1)S(1)}, bf16[256,2048]{0,1:T(8,128)(2,1)S(1)}, u32[]{:S(2)}, u32[]{:S(2)}) collective-permute-start(bf16[256,2048]{0,1:T(8,128)(2,1)S(1)} %get-tuple-element.88), channel_id=1, source_target_pairs={{24,16},{25,17},{26,18},{27,19},{28,20},{29,21},{30,22},{31,23}} | collective-permute-start | bytes 3145736 | tf_op jit(solution)/shard_map/ppermute | solution.py:93
  450.5 40.9 %slice-start = ((s8[5767168]{0:T(1024)(128)(4,1)}), s8[4194304]{0:T(1024)(128)(4,1)S(1)}, s32[]{:S(2)}) async-start(s8[5767168]{0:T(1024)(128)(4,1)} %bitcast.128), calls=%async_computation | async-start | bytes 8388608
  450.5 40.9 %slice-start.1 = ((s8[5767168]{0:T(1024)(128)(4,1)}), s8[1572864]{0:T(1024)(128)(4,1)S(1)}, s32[]{:S(2)}) async-start(s8[5767168]{0:T(1024)(128)(4,1)} %bitcast.128), calls=%async_computation.1 | async-start | bytes 3145728
  450.5 49.8 %collective-permute-start.43 = (bf16[256,2048]{0,1:T(8,128)(2,1)}, bf16[256,2048]{0,1:T(8,128)(2,1)S(1)}, u32[]{:S(2)}, u32[]{:S(2)}) collective-permute-start(bf16[256,2048]{0,1:T(8,128)(2,1)} %get-tuple-element.89), channel_id=1, source_target_pairs={{0,8},{1,9},{2,10},{3,11},{4,12},{5,13},{6,14},{7,15}} | collective-permute-start | bytes 3145736 | tf_op jit(solution)/shard_map/ppermute | solution.py:94
  483.2 354.3 %copy-start.19 = (f32[1024,2048]{0,1:T(8,128)}, f32[1024,2048]{0,1:T(8,128)S(1)}, u32[]{:S(2)}) copy-start(f32[1024,2048]{0,1:T(8,128)S(1)} %convolution_add_fusion) | copy-start | bytes 25165828
  484.7 12.9 %collective-permute-start.31 = (bf16[256,2048]{0,1:T(8,128)(2,1)}, bf16[256,2048]{0,1:T(8,128)(2,1)}, u32[]{:S(2)}, u32[]{:S(2)}) collective-permute-start(bf16[256,2048]{0,1:T(8,128)(2,1)} %get-tuple-element.92), channel_id=1, source_target_pairs={{24,16},{25,17},{26,18},{27,19},{28,20},{29,21},{30,22},{31,23}} | collective-permute-start | bytes 3145736 | tf_op jit(solution)/shard_map/ppermute | solution.py:93
  489.7 11.6 %collective-permute-start.41 = (bf16[256,2048]{0,1:T(8,128)(2,1)}, bf16[256,2048]{0,1:T(8,128)(2,1)}, u32[]{:S(2)}, u32[]{:S(2)}) collective-permute-start(bf16[256,2048]{0,1:T(8,128)(2,1)} %add_convert_fusion.3), channel_id=1, source_target_pairs={{16,8},{24,16},{17,9},{25,17},{18,10},{26,18},{19,11},{27,19},{20,... | collective-permute-start | bytes 3145736 | tf_op jit(solution)/shard_map/ppermute | solution.py:93
  496.0 40.7 %copy-start.18 = (bf16[1024,2048]{0,1:T(8,128)(2,1)S(1)}, bf16[1024,2048]{0,1:T(8,128)(2,1)}, u32[]{:S(2)}) copy-start(bf16[1024,2048]{0,1:T(8,128)(2,1)} %copy-done.15) | copy-start | bytes 12582916
  496.0 48.3 %collective-permute-start.34 = (bf16[256,2048]{0,1:T(8,128)(2,1)S(1)}, bf16[256,2048]{0,1:T(8,128)(2,1)S(1)}, u32[]{:S(2)}, u32[]{:S(2)}) collective-permute-start(bf16[256,2048]{0,1:T(8,128)(2,1)S(1)} %get-tuple-element.93), channel_id=1, source_target_pairs={{0,8},{1,9},{2,10},{3,11},{4,12},{5,13},{6,14},{7,15}} | collective-permute-start | bytes 3145736 | tf_op jit(solution)/shard_map/ppermute | solution.py:94
  499.2 45.1 %collective-permute-start.32 = (bf16[256,2048]{0,1:T(8,128)(2,1)S(1)}, bf16[256,2048]{0,1:T(8,128)(2,1)S(1)}, u32[]{:S(2)}, u32[]{:S(2)}) collective-permute-start(bf16[256,2048]{0,1:T(8,128)(2,1)S(1)} %add_convert_fusion.7), channel_id=1, source_target_pairs={{16,8},{24,16},{17,9},{25,17},{18,10},{26,18},{19,11},{27,19},{20,... | collective-permute-start | bytes 3145736 | tf_op jit(solution)/shard_map/ppermute | solution.py:93
  504.7 61.7 %collective-permute-start.44 = (bf16[256,2048]{0,1:T(8,128)(2,1)S(1)}, bf16[256,2048]{0,1:T(8,128)(2,1)S(1)}, u32[]{:S(2)}, u32[]{:S(2)}) collective-permute-start(bf16[256,2048]{0,1:T(8,128)(2,1)S(1)} %get-tuple-element.87), channel_id=1, source_target_pairs={{8,16},{0,8},{9,17},{1,9},{10,18},{2,10},{11,19},{3,11},{12,20},{4... | collective-permute-start | bytes 3145736 | tf_op jit(solution)/shard_map/ppermute | solution.py:94
  543.0 351.2 %collective-permute-start.42 = (bf16[256,2048]{0,1:T(8,128)(2,1)S(1)}, bf16[256,2048]{0,1:T(8,128)(2,1)}, u32[]{:S(2)}, u32[]{:S(2)}) collective-permute-start(bf16[256,2048]{0,1:T(8,128)(2,1)S(1)} %get-tuple-element.86), channel_id=1, source_target_pairs={{8,0},{16,8},{24,16},{9,1},{17,9},{25,17},{10,2},{18,10},{26,18},{... | collective-permute-start | bytes 3145736 | tf_op jit(solution)/shard_map/ppermute | solution.py:93
  546.5 291.0 %collective-permute-start.35 = (bf16[256,2048]{0,1:T(8,128)(2,1)}, bf16[256,2048]{0,1:T(8,128)(2,1)}, u32[]{:S(2)}, u32[]{:S(2)}) collective-permute-start(bf16[256,2048]{0,1:T(8,128)(2,1)} %get-tuple-element.91), channel_id=1, source_target_pairs={{8,16},{0,8},{9,17},{1,9},{10,18},{2,10},{11,19},{3,11},{12,20},{4... | collective-permute-start | bytes 3145736 | tf_op jit(solution)/shard_map/ppermute | solution.py:94
  569.2 324.9 %collective-permute-start.45 = (bf16[256,2048]{0,1:T(8,128)(2,1)}, bf16[256,2048]{0,1:T(8,128)(2,1)}, u32[]{:S(2)}, u32[]{:S(2)}) collective-permute-start(bf16[256,2048]{0,1:T(8,128)(2,1)} %add_convert_fusion), channel_id=1, source_target_pairs={{16,24},{8,16},{0,8},{17,25},{9,17},{1,9},{18,26},{10,18},{2,10},{... | collective-permute-start | bytes 3145736 | tf_op jit(solution)/shard_map/ppermute | solution.py:94
  826.0 68.1 %copy-start.22 = (bf16[1,256,2048]{1,2,0:T(8,128)(2,1)S(1)}, bf16[1,256,2048]{1,2,0:T(8,128)(2,1)}, u32[]{:S(2)}) copy-start(bf16[1,256,2048]{1,2,0:T(8,128)(2,1)} %copy.89) | copy-start | bytes 3145732
  826.0 68.1 %copy-start.36 = (f32[256]{0:T(256)S(1)}, f32[256]{0:T(256)}, u32[]{:S(2)}) copy-start(f32[256]{0:T(256)} %copy-done.35) | copy-start | bytes 3076
  826.0 68.2 %copy-start.37 = (f32[256]{0:T(256)S(1)}, f32[256]{0:T(256)}, u32[]{:S(2)}) copy-start(f32[256]{0:T(256)} %add_rsqrt_fusion.1) | copy-start | bytes 3076
  836.3 61.0 %collective-permute-start.33 = (bf16[256,2048]{0,1:T(8,128)(2,1)}, bf16[256,2048]{0,1:T(8,128)(2,1)}, u32[]{:S(2)}, u32[]{:S(2)}) collective-permute-start(bf16[256,2048]{0,1:T(8,128)(2,1)} %get-tuple-element.90), channel_id=1, source_target_pairs={{8,0},{16,8},{24,16},{9,1},{17,9},{25,17},{10,2},{18,10},{26,18},{... | collective-permute-start | bytes 3145736 | tf_op jit(solution)/shard_map/ppermute | solution.py:93
  840.2 57.1 %collective-permute-start.36 = (bf16[256,2048]{0,1:T(8,128)(2,1)}, bf16[256,2048]{0,1:T(8,128)(2,1)}, u32[]{:S(2)}, u32[]{:S(2)}) collective-permute-start(bf16[256,2048]{0,1:T(8,128)(2,1)} %add_convert_fusion.4), channel_id=1, source_target_pairs={{16,24},{8,16},{0,8},{17,25},{9,17},{1,9},{18,26},{10,18},{2,10},{... | collective-permute-start | bytes 3145736 | tf_op jit(solution)/shard_map/ppermute | solution.py:94
  (26 other events, 116.3 us)
